TPU v7x, 32 devices: a whole 2x2x4 slice. The times are simulated.
32 devices in a mesh: grp: 2 (over y), row: 4 (over x, core), col: 4 (over z).
Axes of the slice: x: 2, y: 2, z: 4, core: 2. Of those that a mesh axis runs over, the one named last changes fastest.
Arguments:
- factor: float32 [8, 4, 768, 768], P(('grp', 'row'), 'col'), parts along dimension 0
- rhs: float32 [8, 768, 64], P(('grp', 'row')), parts along dimension 0, may hold values from -6 to 6
- pattern: int32 [8, 4], P('grp'), parts along dimension 0, may hold values from 0 to 1, as said below
Outputs:
- solution: float32 [8, 768, 64], P(('grp', 'col'), 'row'), parts along dimension 0
There are 2 independent parts, one for each index of `grp`. A program takes and returns all parts, laid end to end along the dimension named above; each array names one. Nothing has to cross between parts.
Inputs may be any that keep to these rules, and one draw needn't show every extreme that they name: pattern[i, j] = 1 only where j < i; the blocks form an elimination tree in which every block but the last has exactly one parent p > j with pattern[p, j] = 1, and pattern[i, j] = 1 only where i is an ancestor of j; every chain of blocks linked by pattern has at most 4 blocks and some chain has exactly 4.
All inputs are finite; a program needn't handle non-finite values.
Results may differ from a plain program's by a relative error of at most 0.0001.
Values sent between devices are 32-bit elements; how exact they have to be, the bound alone decides.
No kernel may reach another device: no remote copies, remote signals or barrier semaphores. Data moves between devices by JAX's collectives and lax.ppermute only.
A program may use at most 64 MiB of HBM per device.

v0:
```python
import jax
import jax.numpy as jnp
from jax import lax
from jax.sharding import PartitionSpec as P


def from_root(shard, axis, root):
    mine = lax.axis_index(axis) == root
    return lax.psum(jnp.where(mine, shard, jnp.zeros_like(shard)), axis)


def multiply(factor_tile, columns):
    return jnp.dot(
        factor_tile, columns, precision=lax.Precision.HIGHEST, preferred_element_type=jnp.float32
    )


def advance(factor_tile, right_cols, carried, solve_now, apply_now, final_level):

    def solve_branch(operand):
        return multiply(factor_tile, operand)

    def empty_branch(operand):
        return jnp.zeros_like(operand)

    fresh = lax.cond(solve_now, solve_branch, empty_branch, right_cols - carried)
    arrived = from_root(fresh, "row", lax.axis_index("col"))
    if not final_level:
        product = lax.cond(apply_now, solve_branch, empty_branch, arrived)
        carried = carried + lax.psum(product, "col")
    return (arrived, carried)


def local(factor, rhs, pattern):
    factor_tile = factor[0, 0]
    right_rows = rhs[0]
    here_row = lax.axis_index("row")
    here_col = lax.axis_index("col")
    depth_count = min(6, lax.axis_size("row"))
    linked = pattern == 1
    height = jnp.zeros((pattern.shape[0],), jnp.int32)
    for sweep_index in range(depth_count):
        height = jnp.max(jnp.where(linked, height[None, :] + 1, 0), axis=1)
    own_height = height[here_row]
    column_height = height[here_col]
    on_diagonal = here_row == here_col
    uses_block = pattern[here_row, here_col] == 1
    pieces = [right_rows]
    carried = [jnp.zeros_like(piece) for piece in pieces]
    solved = [jnp.zeros_like(piece) for piece in pieces]
    for level_now in range(depth_count):
        solve_now = on_diagonal & (own_height == level_now)
        apply_now = uses_block & (column_height == level_now)
        arrived, carried[0] = advance(
            factor_tile, pieces[0], carried[0], solve_now, apply_now, level_now == depth_count - 1
        )
        solved[0] = solved[0] + arrived
    solved_all = solved[0]
    own_rows = solved_all.shape[0] // lax.axis_size("row")
    return lax.dynamic_slice_in_dim(solved_all, here_row * own_rows, own_rows, 0)[None]


def solution(mesh):
    in_specs = (P(("grp", "row"), "col", None, None), P(("grp", "row"), None, None), P("grp", None))
    out_specs = P(("grp", "col"), "row", None)
    return jax.shard_map(local, mesh=mesh, in_specs=in_specs, out_specs=out_specs, check_vma=False)
```

profile of v0, /device:TPU:30, one launch (start us, length us, event | category | flops | bytes accessed | tf_op | source)
XLA Modules:
  0.0 275.2 jit_solution(16955222185634692702)
XLA Ops:
  6.5 0.8 select_reduce_fusion.3
  7.3 0.1 select_reduce_fusion.2
  7.5 0.1 select_reduce_fusion.1
  7.6 0.1 select_reduce_fusion
  7.7 0.6 fusion.5
  9.0 1.1 copy.4
  10.1 0.7 broadcast_select_fusion.3
  10.9 1.3 dynamic_slice.13
  13.4 29.1 %all-reduce.8.cloned.1.call-done = f32[768,64]{0,1:T(8,128)} async-done(((f32[768,64]{0,1:T(8,128)}), f32[768,64]{0,1:T(8,128)}) %all-reduce.8.cloned.1.call-update) | async-done | bytes 196624 | tf_op jit(solution)/shard_map/psum | solution.py:9
  42.6 0.9 copy.6
  44.2 37.6 %all-reduce.10.cloned.1.call-done = f32[768,64]{1,0:T(8,128)} async-done(((f32[768,64]{1,0:T(8,128)}), f32[768,64]{1,0:T(8,128)}) %all-reduce.10.cloned.1.call-update) | async-done | bytes 196624 | tf_op jit(solution)/shard_map/psum | solution.py:30
  81.8 0.7 broadcast_select_fusion.2
  83.3 32.5 %all-reduce.12.cloned.1.call-done = f32[768,64]{0,1:T(8,128)} async-done(((f32[768,64]{0,1:T(8,128)}), f32[768,64]{0,1:T(8,128)}) %all-reduce.12.cloned.1.call-update) | async-done | bytes 196624 | tf_op jit(solution)/shard_map/psum | solution.py:9
  115.8 0.9 copy.8
  117.4 38.3 %all-reduce.14.cloned.1.call-done = f32[768,64]{1,0:T(8,128)} async-done(((f32[768,64]{1,0:T(8,128)}), f32[768,64]{1,0:T(8,128)}) %all-reduce.14.cloned.1.call-update) | async-done | bytes 196624 | tf_op jit(solution)/shard_map/psum | solution.py:30
  155.7 1.0 add.71
  156.8 0.7 broadcast_select_fusion.1
  158.2 34.7 %all-reduce.16.cloned.1.call-done = f32[768,64]{0,1:T(8,128)} async-done(((f32[768,64]{0,1:T(8,128)}), f32[768,64]{0,1:T(8,128)}) %all-reduce.16.cloned.1.call-update) | async-done | bytes 196624 | tf_op jit(solution)/shard_map/psum | solution.py:9
  193.0 0.2 conditional.12
  193.2 0.9 copy.10
  194.8 37.8 %all-reduce.18.cloned.1.call-done = f32[768,64]{1,0:T(8,128)} async-done(((f32[768,64]{1,0:T(8,128)}), f32[768,64]{1,0:T(8,128)}) %all-reduce.18.cloned.1.call-update) | async-done | bytes 196624 | tf_op jit(solution)/shard_map/psum | solution.py:30
  232.6 0.7 broadcast_select_fusion
  233.3 33.3 %all-reduce.20.cloned.1.call-done = f32[768,64]{0,1:T(8,128)} async-done(((f32[768,64]{0,1:T(8,128)}), f32[768,64]{0,1:T(8,128)}) %all-reduce.20.cloned.1.call-update) | async-done | bytes 196624 | tf_op jit(solution)/shard_map/psum | solution.py:9
  266.6 1.8 fusion.4
  (32 shorter events, 0.6 us)
Async XLA Ops:
  6.5 36.0 %all-reduce.8.cloned.1.call-start = ((), (), s32[]{:S(2)}) async-start(), calls=%async_computation | async-start | bytes 393216 | tf_op jit(solution)/shard_map/psum | solution.py:9
  10.8 71.0 %all-reduce.10.cloned.1.call-start = ((), (), s32[]{:S(2)}) async-start(), calls=%async_computation.1 | async-start | bytes 786432 | tf_op jit(solution)/shard_map/psum | solution.py:30
  43.5 72.2 %all-reduce.12.cloned.1.call-start = ((), (), s32[]{:S(2)}) async-start(), calls=%async_computation.2 | async-start | bytes 393216 | tf_op jit(solution)/shard_map/psum | solution.py:9
  81.8 73.9 %copy-start = (f32[768,64]{1,0:T(8,128)S(1)}, f32[768,64]{1,0:T(8,128)}, u32[]{:S(2)}) copy-start(f32[768,64]{1,0:T(8,128)} %all-reduce.10.cloned.1.call-done) | copy-start | bytes 589828
  82.6 73.1 %all-reduce.14.cloned.1.call-start = ((), (), s32[]{:S(2)}) async-start(), calls=%async_computation.3 | async-start | bytes 786432 | tf_op jit(solution)/shard_map/psum | solution.py:30
  116.8 76.2 %all-reduce.16.cloned.1.call-start = ((), (), s32[]{:S(2)}) async-start(), calls=%async_computation.4 | async-start | bytes 393216 | tf_op jit(solution)/shard_map/psum | solution.py:9
  157.5 75.0 %all-reduce.18.cloned.1.call-start = ((), (), s32[]{:S(2)}) async-start(), calls=%async_computation.5 | async-start | bytes 786432 | tf_op jit(solution)/shard_map/psum | solution.py:30
  194.1 72.5 %all-reduce.20.cloned.1.call-start = ((), (), s32[]{:S(2)}) async-start(), calls=%async_computation.6 | async-start | bytes 393216 | tf_op jit(solution)/shard_map/psum | solution.py:9
Sparse Core Ops, SparseCore 0:
  10.9 31.5 all-reduce.7
  45.0 36.7 all-reduce.9
  84.1 31.5 all-reduce.11
  118.1 37.5 all-reduce.13
  157.9 35.0 all-reduce.15
  195.3 37.2 all-reduce.17
  234.9 31.6 all-reduce.19
where the time goes:
time: 278 us; the launch traced here: 275 us
  waiting for transfers between devices  243 us (87%)
  between operations  18.7 us (7%)
  other arithmetic  6.79 us (2%)
  local copies, waits for them, and re-layouts  5.86 us (2%)
    psum x4, waiting for transfers between devices, from_root(): return lax.psum(jnp.where(mine, shard, jnp.zeros_like(shard)), axis)  130 us
    psum x3, waiting for transfers between devices, advance(): carried = carried + lax.psum(product, 'col')  114 us
  transfers between devices with their start and end apart: 7, of which 7 were waited for; matrix products, arithmetic and copies ran while one was open for 0% of the time, Pallas kernels for 0%

commit v1 on v0

v1 whole, which is shorter than its diff:
```python
import functools

import jax
import jax.numpy as jnp
from jax import lax
from jax.experimental import pallas as pl
from jax.experimental.pallas import tpu as pltpu
from jax.sharding import PartitionSpec as P

GRID = ("row", "col")
PIECES = 1
LOADS = 6
FLAT = (((1,), (0,)), ((), ()))
TURNED = (((1,), (1,)), ((), ()))
SIDE = 4


def split(values):
    big = values.astype(jnp.bfloat16)
    return big, (values - big.astype(jnp.float32)).astype(jnp.bfloat16)


def product(columns, big, small, dims):
    count = columns.shape[0]
    high, low = split(columns)
    dot = functools.partial(lax.dot_general, dimension_numbers=dims, preferred_element_type=jnp.float32)
    both = dot(jnp.concatenate([high, low], 0), big)
    return both[:count] + (both[count:] + dot(high, small))


def here(row, col):
    return (lax.axis_index("row") == row) & (lax.axis_index("col") == col)


def call(kernel, name, outs, args, spaces=None, scratch=(), flops=0, size=0):
    spaces = spaces or [pltpu.VMEM] * len(args)
    return pl.pallas_call(
        kernel,
        out_shape=outs,
        in_specs=[pl.BlockSpec(memory_space=space) for space in spaces],
        out_specs=jax.tree.map(lambda _: pl.BlockSpec(memory_space=pltpu.VMEM), outs),
        scratch_shapes=scratch,
        compiler_params=pltpu.CompilerParams(vmem_limit_bytes=24 << 20),
        cost_estimate=pl.CostEstimate(flops=flops, bytes_accessed=size, transcendentals=0),
        name=name,
    )(*args)


def like(array, dtype=None, shape=None):
    return jax.ShapeDtypeStruct(shape or array.shape, dtype or array.dtype)


def load_block(factor_hbm, right, pattern, big_ref, small_ref, *rest):
    found, (buffer, sems) = rest[:-2], rest[-2:]
    order = right.shape[1]
    rows = order // LOADS
    copies = [
        pltpu.make_async_copy(factor_hbm.at[pl.ds(k * rows, rows)], buffer.at[pl.ds(k * rows, rows)], sems.at[k])
        for k in range(LOADS)
    ]
    for copy in copies:
        copy.start()
    row, col = lax.axis_index("row"), lax.axis_index("col")
    first = here(0, 0)
    used = (row == col) | (pattern[row, col] == 1)
    for k, copy in enumerate(copies):
        copy.wait()
        part = slice(k * rows, (k + 1) * rows)

        @pl.when(first)
        def _():
            answer = product(right[...], *split(buffer[part]), TURNED)
            count = found[0].shape[0]
            for n, ref in enumerate(found):
                ref[:, part] = answer[n * count : (n + 1) * count]

        @pl.when(jnp.logical_not(first))
        def _():
            block = jnp.where(used, buffer[part], 0.0).T
            big_ref[:, part], small_ref[:, part] = split(block)

    @pl.when(jnp.logical_not(first))
    def _():
        for ref in found:
            ref[...] = jnp.zeros_like(ref)


def load_below(factor, pattern, big_ref, small_ref):
    @pl.when(here(2, 2))
    def _():
        block = jnp.where(pattern[3, 2] == 1, factor[...], 0.0).T
        big_ref[...], small_ref[...] = split(block)


def step_first(big, small, held, got, out):
    out[...] = held[...]

    @pl.when(here(1, 0))
    def _():
        out[...] = product(got[...], big[...], small[...], FLAT)


def step_second(big, small, held, right, early, got, out):
    out[...] = held[...]

    def put(columns):
        out[...] = product(columns, big[...], small[...], FLAT)

    @pl.when(here(1, 1))
    def _():
        put(right[...] - got[...])

    @pl.when(here(2, 0))
    def _():
        put(early[...])

    @pl.when(here(3, 0))
    def _():
        put(got[...])


def step_third(big, small, held, got, out):
    out[...] = held[...]

    @pl.when(here(2, 1))
    def _():
        out[...] = product(got[...], big[...], small[...], FLAT)


def step_beside(big, small, held, got, out):
    out[...] = held[...]

    @pl.when(here(3, 1))
    def _():
        out[...] = product(got[...], big[...], small[...], FLAT)


def step_fourth(big, small, below_big, below_small, held, right, early, got, out, carried):
    out[...] = held[...]
    carried[...] = jnp.zeros_like(carried)

    @pl.when(here(2, 2))
    def _():
        answer = product(right[...] - early[...] - got[...], big[...], small[...], FLAT)
        out[...] = answer
        carried[...] = product(answer, below_big[...], below_small[...], FLAT)


def step_last(big, small, held, right, early, middle, got, out, *shares):
    out[...] = held[...]

    @pl.when(here(3, 3))
    def _():
        columns = right[...] - early[...] - middle[...] - got[...]
        out[...] = product(columns, big[...], small[...], FLAT)

    wide = out.shape[1] // SIDE
    row = lax.axis_index("row")
    for k in range(SIDE):

        @pl.when(row == (k ^ 1))
        def _():
            shares[0][...] = out[:, k * wide : (k + 1) * wide]

    for k in range(2):
        shares[k + 1][...] = out[:, k * wide : (k + 1) * wide]


def give(held, first, early, second, third, beside, across, zero, one, out):
    wide = out.shape[1]
    whole = {
        (0, 0): held, (1, 0): first, (2, 0): early, (3, 0): second,
        (1, 1): held, (2, 1): third, (3, 1): beside,
        (2, 2): held, (3, 3): held,
    }
    share = {(0, 1): across, (3, 2): across, (2, 3): across, (0, 2): zero, (0, 3): zero, (1, 2): one, (1, 3): one}
    for (row, col), ref in whole.items():

        @pl.when(here(row, col))
        def _(row=row, ref=ref):
            out[...] = ref[:, row * wide : (row + 1) * wide]

    for (row, col), ref in share.items():

        @pl.when(here(row, col))
        def _(ref=ref):
            out[...] = ref[...]


def route(*cycles):
    target = {}
    for cycle in cycles:
        for spot, source in enumerate(cycle):
            target[source] = cycle[(spot + 1) % len(cycle)]
    for row in range(SIDE):
        for col in range(SIDE):
            target.setdefault((row, col), (row ^ 1, col))
    assert sorted(target) == sorted(target.values())
    return [(a * SIDE + b, c * SIDE + d) for (a, b), (c, d) in target.items()]


SWAP = route()
EARLY = route([(0, 0), (2, 0), (3, 0), (1, 0)])
SECOND = route([(1, 0), (1, 1), (0, 1), (0, 0), (3, 0), (2, 0)])
THIRD = route([(1, 1), (2, 1), (0, 1)], [(2, 0), (2, 2), (3, 2), (3, 0), (2, 3), (3, 3), (3, 1)])
FOURTH = route([(2, 1), (2, 2)], [(3, 1), (3, 3), (2, 3), (3, 2)])
LAST = route([(2, 2), (3, 3), (2, 3), (3, 2)])
TO_ZERO = route([(3, 3), (0, 3), (1, 3), (2, 3)], [(2, 2), (0, 2), (1, 2), (3, 2)])
TO_ONE = route([(3, 3), (1, 3), (0, 3), (2, 3)], [(2, 2), (1, 2), (0, 2), (3, 2)])
BELOW = [(3 * SIDE + 2, 2 * SIDE + 2)]


def send(pairs, arrays):
    return [lax.ppermute(array, GRID, pairs) for array in arrays]


def chain(factor, rhs, pattern):
    block = factor[0, 0]
    order = block.shape[0]
    right = rhs[0].T
    count = right.shape[0] // PIECES
    pieces = [right[k * count : (k + 1) * count] for k in range(PIECES)]
    half = like(block, jnp.bfloat16)
    vector = like(pieces[0])
    work = 6 * order * order * count

    def each(kernel, name, outs, *lists, shared=()):
        return [
            call(kernel, name, outs, (*shared, *args), flops=work, size=4 * order * order) for args in zip(*lists)
        ]

    big, small, *held = call(
        load_block, "load_block", [half, half] + [vector] * PIECES, (block, right, pattern),
        [pltpu.HBM, pltpu.VMEM, pltpu.SMEM],
        [pltpu.VMEM(block.shape, block.dtype), pltpu.SemaphoreType.DMA((LOADS,))],
        6 * work, 8 * order * order,
    )
    shared = (big, small)
    first = send(SWAP, held)
    (below,) = send(BELOW, [block])
    early = send(EARLY, held)
    held = each(step_first, "step_first", vector, held, first, shared=shared)
    second = send(SECOND, held)
    held = each(step_second, "step_second", vector, held, pieces, early, second, shared=shared)
    third = send(THIRD, held)
    beside = send(SWAP, third)
    held = each(step_third, "step_third", vector, held, third, shared=shared)
    held = each(step_beside, "step_beside", vector, held, beside, shared=shared)
    fourth = send(FOURTH, held)
    under = call(
        load_below, "load_below", [half, half], (below, pattern), [pltpu.VMEM, pltpu.SMEM], flops=work, size=8 * order * order
    )
    pairs = each(step_fourth, "step_fourth", [vector, vector], held, pieces, third, fourth, shared=(*shared, *under))
    held = [pair[0] for pair in pairs]
    last = send(LAST, [pair[1] for pair in pairs])
    share = like(pieces[0], shape=(count, order // SIDE))
    ends = each(step_last, "step_last", [vector] + [share] * 3, held, pieces, beside, fourth, last, shared=shared)
    held = [end[0] for end in ends]
    across = send(SWAP, [end[1] for end in ends])
    zero = send(TO_ZERO, [end[2] for end in ends])
    one = send(TO_ONE, [end[3] for end in ends])
    given = each(give, "give", share, held, first, early, second, third, beside, across, zero, one)
    return jnp.concatenate(given, 0).T[None]


def from_root(shard, axis, root):
    mine = lax.axis_index(axis) == root
    return lax.psum(jnp.where(mine, shard, jnp.zeros_like(shard)), axis)


def multiply(factor_tile, columns):
    return jnp.dot(factor_tile, columns, precision=lax.Precision.HIGHEST, preferred_element_type=jnp.float32)


def levels(factor, rhs, pattern):
    block, right = factor[0, 0], rhs[0]
    row, col = lax.axis_index("row"), lax.axis_index("col")
    depth = min(6, lax.axis_size("row"))
    height = jnp.zeros((pattern.shape[0],), jnp.int32)
    for _ in range(depth):
        height = jnp.max(jnp.where(pattern == 1, height[None, :] + 1, 0), axis=1)
    solved = carried = jnp.zeros_like(right)
    times = functools.partial(multiply, block)
    for level in range(depth):
        solve_now = (row == col) & (height[row] == level)
        fresh = lax.cond(solve_now, times, jnp.zeros_like, right - carried)
        arrived = from_root(fresh, "row", col)
        if level < depth - 1:
            apply_now = (pattern[row, col] == 1) & (height[col] == level)
            carried = carried + lax.psum(lax.cond(apply_now, times, jnp.zeros_like, arrived), "col")
        solved = solved + arrived
    share = solved.shape[0] // lax.axis_size("row")
    return lax.dynamic_slice_in_dim(solved, row * share, share, 0)[None]


def solution(mesh):
    in_specs = (P(("grp", "row"), "col", None, None), P(("grp", "row"), None, None), P("grp", None))
    out_specs = P(("grp", "col"), "row", None)
    local = chain if mesh.shape["row"] == mesh.shape["col"] == SIDE else levels
    return jax.shard_map(local, mesh=mesh, in_specs=in_specs, out_specs=out_specs, check_vma=False)
```

time: 278 us -> 40.1 us (0.14)
  waiting for transfers between devices: 243 us -> 23.4 us
  between operations: 18.7 us -> 0.12 us
  starting transfers between devices: 0.25 us -> 8.34 us
  other arithmetic: 6.79 us -> 0 us
  Pallas kernels: 0 us -> 4.29 us
    psum x7 -> x0, waiting for transfers between devices: 243 us -> none  [the longest x4 130 us: from_root(): return lax.psum(jnp.where(mine, shard, jnp.zeros_like(shard)), axis)]
    ppermute x0 -> x11, waiting for transfers between devices: none -> 23.4 us  [send(): return [lax.ppermute(array, GRID, pairs) for array in arrays]]
    ppermute x0 -> x11, starting transfers between devices: none -> 8.34 us  [send(): return [lax.ppermute(array, GRID, pairs) for array in arrays]]
    pallas_call x0 -> x9, Pallas kernels: none -> 4.29 us  [call(): pl.pallas_call(kernel, out_shape=outs, in_specs=[pl.BlockSpec(memory_spac...]
  transfers between devices with their start and end apart: 7 -> 11, of which waited for: 7 -> 10; matrix products, arithmetic and copies ran while one was open for 0% -> 0% of each run, Pallas kernels for 0% -> 9%
where the time goes in v1:
time: 40.1 us; the launch traced here: 39.4 us
  waiting for transfers between devices  23.4 us (58%)
  starting transfers between devices  8.34 us (21%)
  Pallas kernels  4.29 us (11%)
  local copies, waits for them, and re-layouts  3.28 us (8%)
    ppermute x11, waiting for transfers between devices, send(): return [lax.ppermute(array, GRID, pairs) for array in arrays]  23.4 us
    ppermute x11, starting transfers between devices, send(): return [lax.ppermute(array, GRID, pairs) for array in arrays]  8.34 us
    pallas_call x9, Pallas kernels, call(): pl.pallas_call(kernel, out_shape=outs, in_specs=[pl.BlockSpec(memory_spac...  4.29 us
    unnamed x10, local copies, waits for them, and re-layouts  3.28 us
  transfers between devices with their start and end apart: 11, of which 10 were waited for; matrix products, arithmetic and copies ran while one was open for 0% of the time, Pallas kernels for 9%

profile of v1, /device:TPU:30, one launch (start us, length us, event | category | flops | bytes accessed | tf_op | source)
XLA Modules:
  0.0 39.4 jit_solution(1845196474249096844)
XLA Ops:
  0.0 0.8 %collective-permute-start = (f32[768,768]{1,0:T(8,128)}, f32[768,768]{1,0:T(8,128)S(1)}, u32[]{:S(2)}, u32[]{:S(2)}) collective-permute-start(f32[768,768]{1,0:T(8,128)} %bitcast.11), channel_id=1, source_target_pairs={{14,10},{30,26}} | collective-permute-start | bytes 7077896 | tf_op jit(solution)/shard_map/ppermute | solution.py:214
  0.8 0.9 %copy-done = f32[1,768,64]{1,2,0:T(8,128)S(1)} copy-done((f32[1,768,64]{1,2,0:T(8,128)S(1)}, f32[1,768,64]{1,2,0:T(8,128)}, u32[]{:S(2)}) %copy-start) | copy-done | bytes 196632
  1.7 0.7 %copy-done.2 = s32[4,4]{1,0:T(4,128)S(1)} copy-done((s32[4,4]{1,0:T(4,128)S(1)}, s32[4,4]{1,0:T(4,128)}, u32[]{:S(2)}) %copy-start.2) | copy-done | bytes 88
  2.4 1.7 %copy-done.4 = f32[1,1,768,768]{3,2,1,0:T(8,128)S(1)} copy-done((f32[1,1,768,768]{3,2,1,0:T(8,128)S(1)}, f32[1,1,768,768]{3,2,1,0:T(8,128)}, u32[]{:S(2)}) %copy-start.4) | copy-done | bytes 2359320
  4.1 2.8 %load_block.1 = (bf16[768,768]{1,0:T(8,128)(2,1)S(1)}, bf16[768,768]{1,0:T(8,128)(2,1)S(1)}, f32[64,768]{1,0:T(8,128)S(1)}) custom-call(f32[768,768]{1,0:T(8,128)S(1)} %bitcast.12, f32[64,768]{1,0:T(8,128)S(1)} %bitcast.7, s32[4,4]{1,0:T(4,128)S(1)} %copy-done.2), custom_call_target="tpu_custom_call" | custom-call | flops 1358954496 | bytes 4718592 | tf_op jit(solution)/shard_map/load_block/pallas_call | solution.py:37
  7.0 0.5 %collective-permute-start.2 = (f32[64,768]{1,0:T(8,128)S(1)}, f32[64,768]{1,0:T(8,128)S(1)}, u32[]{:S(2)}, u32[]{:S(2)}) collective-permute-start(f32[64,768]{1,0:T(8,128)S(1)} %get-tuple-element.20.held), channel_id=1, source_target_pairs={{0,8},{8,12},{12,4},{4,0},{1,5},{2,6},{3,7},{5,1},{6,2},{7,3},{9,1... | collective-permute-start | bytes 589832 | tf_op jit(solution)/shard_map/ppermute | solution.py:214
  7.5 0.9 %collective-permute-done.1.got.first = f32[64,768]{1,0:T(8,128)S(1)} collective-permute-done((f32[64,768]{1,0:T(8,128)S(1)}, f32[64,768]{1,0:T(8,128)S(1)}, u32[]{:S(2)}, u32[]{:S(2)}) %collective-permute-start.1) | collective-permute-done | bytes 196640 | tf_op jit(solution)/shard_map/ppermute | solution.py:214
  8.4 0.2 collective-permute-start.3
  8.7 1.2 %collective-permute-done.3.got.second = f32[64,768]{1,0:T(8,128)S(1)} collective-permute-done((f32[64,768]{1,0:T(8,128)S(1)}, f32[64,768]{1,0:T(8,128)S(1)}, u32[]{:S(2)}, u32[]{:S(2)}) %collective-permute-start.3) | collective-permute-done | bytes 196640 | tf_op jit(solution)/shard_map/ppermute | solution.py:214
  9.9 0.2 collective-permute-start.4
  10.1 9.8 %collective-permute-done.4.got.early.third = f32[64,768]{1,0:T(8,128)S(1)} collective-permute-done((f32[64,768]{1,0:T(8,128)S(1)}, f32[64,768]{1,0:T(8,128)S(1)}, u32[]{:S(2)}, u32[]{:S(2)}) %collective-permute-start.4) | collective-permute-done | bytes 196640 | tf_op jit(solution)/shard_map/ppermute | solution.py:214
  20.0 1.4 %collective-permute-done.5.got.early.beside = f32[64,768]{1,0:T(8,128)S(1)} collective-permute-done((f32[64,768]{1,0:T(8,128)S(1)}, f32[64,768]{1,0:T(8,128)S(1)}, u32[]{:S(2)}, u32[]{:S(2)}) %collective-permute-start.5) | collective-permute-done | bytes 196640 | tf_op jit(solution)/shard_map/ppermute | solution.py:214
  21.5 0.6 %load_below.1 = (bf16[768,768]{1,0:T(8,128)(2,1)S(1)}, bf16[768,768]{1,0:T(8,128)(2,1)S(1)}) custom-call(f32[768,768]{1,0:T(8,128)S(1)} %collective-permute-done.factor, s32[4,4]{1,0:T(4,128)S(1)} %copy-done.3), custom_call_target="tpu_custom_call" | custom-call | flops 226492416 | bytes 4718592 | tf_op jit(solution)/shard_map/load_below/pallas_call | solution.py:37
  22.1 2.6 %collective-permute-done.6.got.middle = f32[64,768]{1,0:T(8,128)S(1)} collective-permute-done((f32[64,768]{1,0:T(8,128)S(1)}, f32[64,768]{1,0:T(8,128)S(1)}, u32[]{:S(2)}, u32[]{:S(2)}) %collective-permute-start.6) | collective-permute-done | bytes 196640 | tf_op jit(solution)/shard_map/ppermute | solution.py:214
  24.7 2.3 %collective-permute-start.7 = (f32[64,768]{1,0:T(8,128)S(1)}, f32[64,768]{1,0:T(8,128)S(1)}, u32[]{:S(2)}, u32[]{:S(2)}) collective-permute-start(f32[64,768]{1,0:T(8,128)S(1)} %get-tuple-element.22), channel_id=1, source_target_pairs={{10,15},{15,11},{11,14},{14,10},{0,4},{1,5},{2,6},{3,7},{4,0},{5,1... | collective-permute-start | bytes 589832 | tf_op jit(solution)/shard_map/ppermute | solution.py:214
  27.0 3.2 %collective-permute-done.7.got = f32[64,768]{1,0:T(8,128)S(1)} collective-permute-done((f32[64,768]{1,0:T(8,128)S(1)}, f32[64,768]{1,0:T(8,128)S(1)}, u32[]{:S(2)}, u32[]{:S(2)}) %collective-permute-start.7) | collective-permute-done | bytes 196640 | tf_op jit(solution)/shard_map/ppermute | solution.py:214
  30.1 0.2 step_last.1
  30.3 4.1 %collective-permute-start.8 = (f32[64,192]{1,0:T(8,128)S(1)}, f32[64,192]{1,0:T(8,128)S(1)}, u32[]{:S(2)}, u32[]{:S(2)}) collective-permute-start(f32[64,192]{1,0:T(8,128)S(1)} %get-tuple-element.24), channel_id=1, source_target_pairs={{0,4},{1,5},{2,6},{3,7},{4,0},{5,1},{6,2},{7,3},{8,12},{9,13},{10,... | collective-permute-start | bytes 147464 | tf_op jit(solution)/shard_map/ppermute | solution.py:214
  34.4 0.1 collective-permute-start.9
  34.5 0.1 collective-permute-start.10
  34.6 0.7 %collective-permute-done.8.across = f32[64,192]{1,0:T(8,128)S(1)} collective-permute-done((f32[64,192]{1,0:T(8,128)S(1)}, f32[64,192]{1,0:T(8,128)S(1)}, u32[]{:S(2)}, u32[]{:S(2)}) %collective-permute-start.8) | collective-permute-done | bytes 49184 | tf_op jit(solution)/shard_map/ppermute | solution.py:214
  35.3 2.9 %collective-permute-done.9.zero = f32[64,192]{1,0:T(8,128)S(1)} collective-permute-done((f32[64,192]{1,0:T(8,128)S(1)}, f32[64,192]{1,0:T(8,128)S(1)}, u32[]{:S(2)}, u32[]{:S(2)}) %collective-permute-start.9) | collective-permute-done | bytes 49184 | tf_op jit(solution)/shard_map/ppermute | solution.py:214
  38.2 0.6 %collective-permute-done.10.one = f32[64,192]{1,0:T(8,128)S(1)} collective-permute-done((f32[64,192]{1,0:T(8,128)S(1)}, f32[64,192]{1,0:T(8,128)S(1)}, u32[]{:S(2)}, u32[]{:S(2)}) %collective-permute-start.10) | collective-permute-done | bytes 49184 | tf_op jit(solution)/shard_map/ppermute | solution.py:214
  38.8 0.6 %give.1 = f32[64,192]{1,0:T(8,128)} custom-call(f32[64,768]{1,0:T(8,128)S(1)} %get-tuple-element.23.held, f32[64,768]{1,0:T(8,128)S(1)} %collective-permute-done.1.got.first, f32[64,768]{1,0:T(8,128)S(1)} %collective-permute-done.2.early, f32[64,768]{1,0:T(8,128)S(1)} %collective-permute-done.3.got.second, ...), custom_call_target="tpu_custom_call" | custom-call | flops 226492416 | bytes 2359296 | tf_op jit(solution)/shard_map/give/pallas_call | solution.py:37
  (17 shorter events, 0.3 us)
Async XLA Ops:
  0.0 21.5 %collective-permute-start = (f32[768,768]{1,0:T(8,128)}, f32[768,768]{1,0:T(8,128)S(1)}, u32[]{:S(2)}, u32[]{:S(2)}) collective-permute-start(f32[768,768]{1,0:T(8,128)} %bitcast.11), channel_id=1, source_target_pairs={{14,10},{30,26}} | collective-permute-start | bytes 7077896 | tf_op jit(solution)/shard_map/ppermute | solution.py:214
  0.8 0.9 %copy-start = (f32[1,768,64]{1,2,0:T(8,128)S(1)}, f32[1,768,64]{1,2,0:T(8,128)}, u32[]{:S(2)}) copy-start(f32[1,768,64]{1,2,0:T(8,128)} %param.4) | copy-start | bytes 589828
  1.7 0.7 %copy-start.2 = (s32[4,4]{1,0:T(4,128)S(1)}, s32[4,4]{1,0:T(4,128)}, u32[]{:S(2)}) copy-start(s32[4,4]{1,0:T(4,128)} %pattern.3) | copy-start | bytes 196
  2.4 1.7 %copy-start.4 = (f32[1,1,768,768]{3,2,1,0:T(8,128)S(1)}, f32[1,1,768,768]{3,2,1,0:T(8,128)}, u32[]{:S(2)}) copy-start(f32[1,1,768,768]{3,2,1,0:T(8,128)} %param.3) | copy-start | bytes 7077892
  6.9 1.5 %collective-permute-start.1 = (f32[64,768]{1,0:T(8,128)S(1)}, f32[64,768]{1,0:T(8,128)S(1)}, u32[]{:S(2)}, u32[]{:S(2)}) collective-permute-start(f32[64,768]{1,0:T(8,128)S(1)} %get-tuple-element.20.held), channel_id=1, source_target_pairs={{0,4},{1,5},{2,6},{3,7},{4,0},{5,1},{6,2},{7,3},{8,12},{9,13},{10,... | collective-permute-start | bytes 589832 | tf_op jit(solution)/shard_map/ppermute | solution.py:214
  7.0 1.7 %collective-permute-start.2 = (f32[64,768]{1,0:T(8,128)S(1)}, f32[64,768]{1,0:T(8,128)S(1)}, u32[]{:S(2)}, u32[]{:S(2)}) collective-permute-start(f32[64,768]{1,0:T(8,128)S(1)} %get-tuple-element.20.held), channel_id=1, source_target_pairs={{0,8},{8,12},{12,4},{4,0},{1,5},{2,6},{3,7},{5,1},{6,2},{7,3},{9,1... | collective-permute-start | bytes 589832 | tf_op jit(solution)/shard_map/ppermute | solution.py:214
  8.4 1.5 %copy-start.1 = (f32[1,768,64]{1,2,0:T(8,128)S(1)}, f32[1,768,64]{1,2,0:T(8,128)}, u32[]{:S(2)}) copy-start(f32[1,768,64]{1,2,0:T(8,128)} %param.4) | copy-start | bytes 589828
  8.4 1.5 %collective-permute-start.3 = (f32[64,768]{1,0:T(8,128)S(1)}, f32[64,768]{1,0:T(8,128)S(1)}, u32[]{:S(2)}, u32[]{:S(2)}) collective-permute-start(f32[64,768]{1,0:T(8,128)S(1)} %step_first.1.held), channel_id=1, source_target_pairs={{4,5},{5,1},{1,0},{0,12},{12,8},{8,4},{2,6},{3,7},{6,2},{7,3},{9,1... | collective-permute-start | bytes 589832 | tf_op jit(solution)/shard_map/ppermute | solution.py:214
  9.9 10.0 %collective-permute-start.4 = (f32[64,768]{1,0:T(8,128)S(1)}, f32[64,768]{1,0:T(8,128)S(1)}, u32[]{:S(2)}, u32[]{:S(2)}) collective-permute-start(f32[64,768]{1,0:T(8,128)S(1)} %step_second.1.held), channel_id=1, source_target_pairs={{5,9},{9,1},{1,5},{8,10},{10,14},{14,12},{12,11},{11,15},{15,13},{... | collective-permute-start | bytes 589832 | tf_op jit(solution)/shard_map/ppermute | solution.py:214
  19.9 1.4 %collective-permute-start.5 = (f32[64,768]{1,0:T(8,128)S(1)}, f32[64,768]{1,0:T(8,128)S(1)}, u32[]{:S(2)}, u32[]{:S(2)}) collective-permute-start(f32[64,768]{1,0:T(8,128)S(1)} %collective-permute-done.4.got.early.third), channel_id=1, source_target_pairs={{0,4},{1,5},{2,6},{3,7},{4,0},{5,1},{6,2},{7,3},{8,12},{9,13},{10,... | collective-permute-start | bytes 589832 | tf_op jit(solution)/shard_map/ppermute | solution.py:214
  20.0 1.5 %copy-start.3 = (s32[4,4]{1,0:T(4,128)S(1)}, s32[4,4]{1,0:T(4,128)}, u32[]{:S(2)}) copy-start(s32[4,4]{1,0:T(4,128)} %pattern.3) | copy-start | bytes 196
  21.4 3.2 %collective-permute-start.6 = (f32[64,768]{1,0:T(8,128)S(1)}, f32[64,768]{1,0:T(8,128)S(1)}, u32[]{:S(2)}, u32[]{:S(2)}) collective-permute-start(f32[64,768]{1,0:T(8,128)S(1)} %step_beside.1.held), channel_id=1, source_target_pairs={{9,10},{10,9},{13,15},{15,11},{11,14},{14,13},{0,4},{1,5},{2,6},{3... | collective-permute-start | bytes 589832 | tf_op jit(solution)/shard_map/ppermute | solution.py:214
  24.7 5.5 %collective-permute-start.7 = (f32[64,768]{1,0:T(8,128)S(1)}, f32[64,768]{1,0:T(8,128)S(1)}, u32[]{:S(2)}, u32[]{:S(2)}) collective-permute-start(f32[64,768]{1,0:T(8,128)S(1)} %get-tuple-element.22), channel_id=1, source_target_pairs={{10,15},{15,11},{11,14},{14,10},{0,4},{1,5},{2,6},{3,7},{4,0},{5,1... | collective-permute-start | bytes 589832 | tf_op jit(solution)/shard_map/ppermute | solution.py:214
  30.3 5.0 %collective-permute-start.8 = (f32[64,192]{1,0:T(8,128)S(1)}, f32[64,192]{1,0:T(8,128)S(1)}, u32[]{:S(2)}, u32[]{:S(2)}) collective-permute-start(f32[64,192]{1,0:T(8,128)S(1)} %get-tuple-element.24), channel_id=1, source_target_pairs={{0,4},{1,5},{2,6},{3,7},{4,0},{5,1},{6,2},{7,3},{8,12},{9,13},{10,... | collective-permute-start | bytes 147464 | tf_op jit(solution)/shard_map/ppermute | solution.py:214
  34.4 3.8 %collective-permute-start.9 = (f32[64,192]{1,0:T(8,128)S(1)}, f32[64,192]{1,0:T(8,128)S(1)}, u32[]{:S(2)}, u32[]{:S(2)}) collective-permute-start(f32[64,192]{1,0:T(8,128)S(1)} %get-tuple-element.25), channel_id=1, source_target_pairs={{15,3},{3,7},{7,11},{11,15},{10,2},{2,6},{6,14},{14,10},{0,4},{1,5... | collective-permute-start | bytes 147464 | tf_op jit(solution)/shard_map/ppermute | solution.py:214
  34.5 4.3 %collective-permute-start.10 = (f32[64,192]{1,0:T(8,128)S(1)}, f32[64,192]{1,0:T(8,128)S(1)}, u32[]{:S(2)}, u32[]{:S(2)}) collective-permute-start(f32[64,192]{1,0:T(8,128)S(1)} %get-tuple-element.26), channel_id=1, source_target_pairs={{15,7},{7,3},{3,11},{11,15},{10,6},{6,2},{2,14},{14,10},{0,4},{1,5... | collective-permute-start | bytes 147464 | tf_op jit(solution)/shard_map/ppermute | solution.py:214

commit v2 on v1

v2 whole, which is shorter than its diff:
```python
import functools

import jax
import jax.numpy as jnp
from jax import lax
from jax.experimental import pallas as pl
from jax.experimental.pallas import tpu as pltpu
from jax.sharding import PartitionSpec as P

GRID = ("row", "col")
LOADS = 3
FLAT = (((1,), (0,)), ((), ()))
TURNED = (((1,), (1,)), ((), ()))
SIDE = 4


def split(values):
    big = values.astype(jnp.bfloat16)
    return big, (values - big.astype(jnp.float32)).astype(jnp.bfloat16)


def product(columns, big, small, dims):
    count = columns.shape[0]
    high, low = split(columns)
    dot = functools.partial(lax.dot_general, dimension_numbers=dims, preferred_element_type=jnp.float32)
    both = dot(jnp.concatenate([high, low], 0), big)
    return both[:count] + (both[count:] + dot(high, small))


def here(row, col):
    return (lax.axis_index("row") == row) & (lax.axis_index("col") == col)


def call(kernel, name, outs, args, spaces=None, scratch=(), flops=0, size=0):
    spaces = spaces or [pltpu.VMEM] * len(args)
    many = isinstance(outs, list)
    kept = [pltpu.VMEM(out.shape, out.dtype) for out in (outs if many else [outs])]
    args = [pltpu.with_memory_space_constraint(a, s) if s is pltpu.HBM else a for a, s in zip(args, spaces)]
    found = pl.pallas_call(
        kernel,
        out_shape=kept,
        in_specs=[pl.BlockSpec(memory_space=space) for space in spaces],
        out_specs=[pl.BlockSpec(memory_space=pltpu.VMEM)] * len(kept),
        scratch_shapes=scratch,
        compiler_params=pltpu.CompilerParams(vmem_limit_bytes=24 << 20),
        cost_estimate=pl.CostEstimate(flops=flops, bytes_accessed=size, transcendentals=0),
        name=name,
    )(*args)
    return found if many else found[0]


def like(array, dtype=None, shape=None):
    return jax.ShapeDtypeStruct(shape or array.shape, dtype or array.dtype)


def fetch(factor_hbm, pattern_hbm, buffer, links, sems):
    rows = buffer.shape[0] // LOADS
    copies = [pltpu.make_async_copy(pattern_hbm, links, sems.at[LOADS])]
    for k in range(LOADS):
        part = pl.ds(k * rows, rows)
        copies.append(pltpu.make_async_copy(factor_hbm.at[part], buffer.at[part], sems.at[k]))
    for copy in copies:
        copy.start()
    return copies


def turn_block(copies, buffer, links, big_ref, small_ref):
    row, col = lax.axis_index("row"), lax.axis_index("col")
    copies[0].wait()
    used = (row == col) | (links[row, col] == 1)
    rows = buffer.shape[0] // LOADS
    for k in range(LOADS):
        copies[k + 1].wait()
        part = slice(k * rows, (k + 1) * rows)
        big_ref[:, part], small_ref[:, part] = split(jnp.where(used, buffer[part], 0.0).T)


def open_chain(factor_hbm, right_hbm, pattern_hbm, right, big_ref, small_ref, found, buffer, links, sems):
    load = pltpu.make_async_copy(right_hbm, right, sems.at[LOADS + 1])
    load.start()

    @pl.when(here(0, 0))
    def _():
        copies = fetch(factor_hbm, pattern_hbm, buffer, links, sems)
        load.wait()
        rows = buffer.shape[0] // LOADS
        for k in range(LOADS):
            copies[k + 1].wait()
            part = slice(k * rows, (k + 1) * rows)
            found[:, part] = product(right[...], *split(buffer[part]), TURNED)
        copies[0].wait()

    @pl.when(here(1, 0))
    def _():
        turn_block(fetch(factor_hbm, pattern_hbm, buffer, links, sems), buffer, links, big_ref, small_ref)

    @pl.when(jnp.logical_not(here(0, 0)))
    def _():
        load.wait()
        found[...] = jnp.zeros_like(found)


def load_block(factor_hbm, pattern_hbm, after, big_ref, small_ref, buffer, links, sems):
    row, col = lax.axis_index("row"), lax.axis_index("col")

    @pl.when((row >= col) & jnp.logical_not(here(0, 0) | here(1, 0)))
    def _():
        turn_block(fetch(factor_hbm, pattern_hbm, buffer, links, sems), buffer, links, big_ref, small_ref)


def advance(rules, plain, big, small, held, *refs):
    sources, out = refs[:-1], refs[-1]
    out[...] = held[...]
    for spot in sorted({*rules, *plain}):

        @pl.when(here(*spot))
        def _(spot=spot):
            given = [source[...] for source in sources]
            terms = [product(rules[spot](*given), big[...], small[...], FLAT)] if spot in rules else []
            terms += [plain[spot](*given)] if spot in plain else []
            out[...] = sum(terms[1:], terms[0])


def share_of(ref, row):
    wide = ref.shape[1] // SIDE
    return ref[:, row * wide : (row + 1) * wide]


def step_two(big, small, held, third, out, aside):
    out[...] = held[...]
    aside[...] = held[...]

    @pl.when(here(2, 1) | here(3, 0))
    def _():
        out[...] = product(third[...], big[...], small[...], FLAT)

    @pl.when(here(2, 1))
    def _():
        aside[...] = third[...]


def pass_two(big, small, held, right, early, got, out, zero, one):
    out[...] = held[...]

    @pl.when(here(2, 2))
    def _():
        out[...] = product(right[...] - early[...] - got[...], big[...], small[...], FLAT)

    zero[...] = share_of(out, 0)
    one[...] = share_of(out, 1)


def close_chain(big, small, held, right, middle, got, out, across, zero, one):
    out[...] = held[...]

    @pl.when(here(3, 3))
    def _():
        columns = right[...] - middle[...] - got[...]
        out[...] = product(columns, big[...], small[...], FLAT)

    row = lax.axis_index("row")
    for k in range(SIDE):

        @pl.when(row == (k ^ 1))
        def _():
            across[...] = share_of(out, k)

    zero[...] = share_of(out, 0)
    one[...] = share_of(out, 1)


def give(held, first, second, third, beside, inside, across, zero_two, one_two, zero, one, out):
    whole = {
        (0, 0): held, (1, 0): first, (2, 0): second, (3, 0): third,
        (1, 1): held, (2, 1): third, (3, 1): beside,
        (2, 2): held, (3, 2): inside, (3, 3): held,
    }
    share = {
        (0, 1): across, (2, 3): across,
        (0, 2): zero_two, (1, 2): one_two, (0, 3): zero, (1, 3): one,
    }
    for (row, col), ref in whole.items():

        @pl.when(here(row, col))
        def _(row=row, ref=ref):
            out[...] = share_of(ref, row)

    for (row, col), ref in share.items():

        @pl.when(here(row, col))
        def _(ref=ref):
            out[...] = ref[...]


def route(*cycles):
    target = {}
    for cycle in cycles:
        for spot, source in enumerate(cycle):
            target[source] = cycle[(spot + 1) % len(cycle)]
    for row in range(SIDE):
        for col in range(SIDE):
            target.setdefault((row, col), (row ^ 1, col))
    assert sorted(target) == sorted(target.values())
    return [(a * SIDE + b, c * SIDE + d) for (a, b), (c, d) in target.items()]


SWAP = route()
TO_11 = route([(1, 0), (1, 1), (0, 1), (0, 0), (2, 0), (3, 0)])
TO_21 = route([(1, 1), (2, 1), (0, 1)], [(0, 0), (3, 0), (2, 0), (3, 1), (1, 0)])
TO_22 = route([(2, 1), (2, 2), (3, 2), (2, 0), (3, 0), (3, 1)])
BESIDE = route([(2, 1), (3, 1)], [(2, 0), (2, 2), (3, 2), (1, 2), (0, 2), (3, 0)])
MIDDLE = route([(3, 1), (3, 3), (2, 3), (2, 1)])
TO_33 = route([(3, 2), (3, 3), (2, 3), (2, 2)])
TO_02 = route([(2, 2), (0, 2)], [(3, 2), (1, 2)])
TO_12 = route([(2, 2), (1, 2)], [(3, 2), (0, 2)])
TO_03 = route([(3, 3), (0, 3), (1, 3), (2, 3)])
TO_13 = route([(3, 3), (1, 3), (0, 3), (2, 3)])


def send(pairs, array):
    return lax.ppermute(array, GRID, pairs)


def chain(factor, rhs, pattern):
    block = factor[0, 0]
    order = block.shape[0]
    turned = rhs[0].T
    half, vector = like(block, jnp.bfloat16), like(turned)
    work = 6 * order * order * turned.shape[0]
    weight = dict(flops=work, size=4 * order * order)
    buffers = [pltpu.VMEM(block.shape, block.dtype), pltpu.SMEM(pattern.shape, pattern.dtype)]

    def move(name, rules, held, *sources, shared, plain={}):
        return call(functools.partial(advance, rules, plain), name, vector, (*shared, held, *sources), **weight)

    right, big, small, held = call(
        open_chain, "open_chain", [vector, half, half, vector], (block, turned, pattern), [pltpu.HBM] * 3,
        buffers + [pltpu.SemaphoreType.DMA((LOADS + 2,))], **weight,
    )
    first = send(SWAP, held)
    carried = move("product_10", {(1, 0): lambda first: first}, held, first, shared=(big, small))
    second = send(TO_11, carried)
    shared = call(
        load_block, "load_block", [half, half], (block, pattern, carried), [pltpu.HBM, pltpu.HBM, pltpu.VMEM],
        buffers + [pltpu.SemaphoreType.DMA((LOADS + 1,))], **weight,
    )
    rules = {(1, 1): lambda right, second: right - second, (2, 0): lambda right, second: second}
    held = move("solve_1", rules, held, right, second, shared=shared)
    third = send(TO_21, held)
    carried, aside = call(step_two, "product_21", [vector, vector], (*shared, held, third), **weight)
    fourth, beside = send(TO_22, carried), send(BESIDE, aside)
    middle = move(
        "product_31", {(3, 1): lambda beside, fourth: beside}, carried, beside, fourth, shared=shared,
        plain={(3, 1): lambda beside, fourth: fourth},
    )
    middle = send(MIDDLE, middle)
    share = like(turned, shape=(turned.shape[0], order // SIDE))
    held, zero_two, one_two = call(
        pass_two, "solve_2", [vector, share, share], (*shared, held, right, beside, fourth), **weight
    )
    inside = send(SWAP, held)
    carried = move("product_32", {(3, 2): lambda got: got}, carried, inside, shared=shared)
    last = send(TO_33, carried)
    zero_two, one_two = send(TO_02, zero_two), send(TO_12, one_two)
    held, across, zero, one = call(
        close_chain, "solve_3", [vector] + [share] * 3, (*shared, held, right, middle, last), **weight
    )
    across, zero, one = send(SWAP, across), send(TO_03, zero), send(TO_13, one)
    given = call(give, "give", share, (held, first, second, third, beside, inside, across, zero_two, one_two, zero, one))
    return given.T[None]


def from_root(shard, axis, root):
    mine = lax.axis_index(axis) == root
    return lax.psum(jnp.where(mine, shard, jnp.zeros_like(shard)), axis)


def multiply(factor_tile, columns):
    return jnp.dot(factor_tile, columns, precision=lax.Precision.HIGHEST, preferred_element_type=jnp.float32)


def levels(factor, rhs, pattern):
    block, right = factor[0, 0], rhs[0]
    row, col = lax.axis_index("row"), lax.axis_index("col")
    depth = min(6, lax.axis_size("row"))
    height = jnp.zeros((pattern.shape[0],), jnp.int32)
    for _ in range(depth):
        height = jnp.max(jnp.where(pattern == 1, height[None, :] + 1, 0), axis=1)
    solved = carried = jnp.zeros_like(right)
    times = functools.partial(multiply, block)
    for level in range(depth):
        solve_now = (row == col) & (height[row] == level)
        fresh = lax.cond(solve_now, times, jnp.zeros_like, right - carried)
        arrived = from_root(fresh, "row", col)
        if level < depth - 1:
            apply_now = (pattern[row, col] == 1) & (height[col] == level)
            carried = carried + lax.psum(lax.cond(apply_now, times, jnp.zeros_like, arrived), "col")
        solved = solved + arrived
    share = solved.shape[0] // lax.axis_size("row")
    return lax.dynamic_slice_in_dim(solved, row * share, share, 0)[None]


def solution(mesh):
    in_specs = (P(("grp", "row"), "col", None, None), P(("grp", "row"), None, None), P("grp", None))
    out_specs = P(("grp", "col"), "row", None)
    local = chain if mesh.shape["row"] == mesh.shape["col"] == SIDE else levels
    return jax.shard_map(local, mesh=mesh, in_specs=in_specs, out_specs=out_specs, check_vma=False)
```

time: 40.1 us -> 31 us (0.77)
  the two profiles are of different devices: /device:TPU:30 before, /device:TPU:29 now
where the time goes in v2:
time: 31 us; the launch traced here: 30.8 us
  starting transfers between devices  19.7 us (64%)
  waiting for transfers between devices  9.08 us (29%)
  Pallas kernels  1.31 us (4%)
  local copies, waits for them, and re-layouts  0.63 us (2%)
    ppermute x13, starting transfers between devices, send(): return lax.ppermute(array, GRID, pairs)  19.7 us
    ppermute x13, waiting for transfers between devices, send(): return lax.ppermute(array, GRID, pairs)  9.08 us
    pallas_call x10, Pallas kernels, call(): pl.pallas_call(kernel, out_shape=kept, in_specs=[pl.BlockSpec(memory_spac...  1.31 us
    unnamed x1, local copies, waits for them, and re-layouts  0.63 us
  transfers between devices with their start and end apart: 13, of which 9 were waited for; matrix products, arithmetic and copies ran while one was open for 0% of the time, Pallas kernels for 1%

profile of v2, /device:TPU:29, one launch (start us, length us, event | category | flops | bytes accessed | tf_op | source)
XLA Modules:
  0.0 30.8 jit_solution(3248585906304157943)
XLA Ops:
  0.0 1.0 %open_chain.1 = (f32[64,768]{1,0:T(8,128)S(1)}, bf16[768,768]{1,0:T(8,128)(2,1)S(1)}, bf16[768,768]{1,0:T(8,128)(2,1)S(1)}, f32[64,768]{1,0:T(8,128)S(1)}) custom-call(f32[768,768]{1,0:T(8,128)} %bitcast.8, f32[64,768]{1,0:T(8,128)} %bitcast.10, s32[4,4]{1,0:T(4,128)} %pattern_hbm.3), custom_call_target="tpu_custom_call" | custom-call | flops 226492416 | bytes 2359296 | tf_op jit(solution)/shard_map/open_chain/pallas_call | solution.py:39
  1.0 0.7 %collective-permute-start = (f32[64,768]{1,0:T(8,128)S(1)}, f32[64,768]{1,0:T(8,128)S(1)}, u32[]{:S(2)}, u32[]{:S(2)}) collective-permute-start(f32[64,768]{1,0:T(8,128)S(1)} %get-tuple-element.22.held), channel_id=1, source_target_pairs={{0,4},{1,5},{2,6},{3,7},{4,0},{5,1},{6,2},{7,3},{8,12},{9,13},{10,... | collective-permute-start | bytes 589832 | tf_op jit(solution)/shard_map/ppermute | solution.py:221
  1.7 1.1 %collective-permute-done.refs_0_.first = f32[64,768]{1,0:T(8,128)S(1)} collective-permute-done((f32[64,768]{1,0:T(8,128)S(1)}, f32[64,768]{1,0:T(8,128)S(1)}, u32[]{:S(2)}, u32[]{:S(2)}) %collective-permute-start) | collective-permute-done | bytes 196640 | tf_op jit(solution)/shard_map/ppermute | solution.py:221
  2.8 0.4 %collective-permute-start.1 = (f32[64,768]{1,0:T(8,128)S(1)}, f32[64,768]{1,0:T(8,128)S(1)}, u32[]{:S(2)}, u32[]{:S(2)}) collective-permute-start(f32[64,768]{1,0:T(8,128)S(1)} %product_10.1.after), channel_id=1, source_target_pairs={{4,5},{5,1},{1,0},{0,8},{8,12},{12,4},{2,6},{3,7},{6,2},{7,3},{9,1... | collective-permute-start | bytes 589832 | tf_op jit(solution)/shard_map/ppermute | solution.py:221
  3.3 1.0 %collective-permute-done.1.refs_1_.second = f32[64,768]{1,0:T(8,128)S(1)} collective-permute-done((f32[64,768]{1,0:T(8,128)S(1)}, f32[64,768]{1,0:T(8,128)S(1)}, u32[]{:S(2)}, u32[]{:S(2)}) %collective-permute-start.1) | collective-permute-done | bytes 196640 | tf_op jit(solution)/shard_map/ppermute | solution.py:221
  4.3 0.4 %collective-permute-start.2 = (f32[64,768]{1,0:T(8,128)S(1)}, f32[64,768]{1,0:T(8,128)S(1)}, u32[]{:S(2)}, u32[]{:S(2)}) collective-permute-start(f32[64,768]{1,0:T(8,128)S(1)} %solve_1.1.held), channel_id=1, source_target_pairs={{5,9},{9,1},{1,5},{0,12},{12,8},{8,13},{13,4},{4,0},{2,6},{3,7},{6... | collective-permute-start | bytes 589832 | tf_op jit(solution)/shard_map/ppermute | solution.py:221
  4.7 1.1 %collective-permute-done.2.third = f32[64,768]{1,0:T(8,128)S(1)} collective-permute-done((f32[64,768]{1,0:T(8,128)S(1)}, f32[64,768]{1,0:T(8,128)S(1)}, u32[]{:S(2)}, u32[]{:S(2)}) %collective-permute-start.2) | collective-permute-done | bytes 196640 | tf_op jit(solution)/shard_map/ppermute | solution.py:221
  5.9 0.4 %collective-permute-start.3 = (f32[64,768]{1,0:T(8,128)S(1)}, f32[64,768]{1,0:T(8,128)S(1)}, u32[]{:S(2)}, u32[]{:S(2)}) collective-permute-start(f32[64,768]{1,0:T(8,128)S(1)} %get-tuple-element.26), channel_id=1, source_target_pairs={{9,13},{13,9},{8,10},{10,14},{14,6},{6,2},{2,12},{12,8},{0,4},{1,5... | collective-permute-start | bytes 589832 | tf_op jit(solution)/shard_map/ppermute | solution.py:221
  6.3 0.1 collective-permute-start.4
  6.4 0.9 %collective-permute-done.3.early.refs_0_.beside = f32[64,768]{1,0:T(8,128)S(1)} collective-permute-done((f32[64,768]{1,0:T(8,128)S(1)}, f32[64,768]{1,0:T(8,128)S(1)}, u32[]{:S(2)}, u32[]{:S(2)}) %collective-permute-start.3) | collective-permute-done | bytes 196640 | tf_op jit(solution)/shard_map/ppermute | solution.py:221
  7.3 0.4 %collective-permute-done.4.got.refs_1_ = f32[64,768]{1,0:T(8,128)S(1)} collective-permute-done((f32[64,768]{1,0:T(8,128)S(1)}, f32[64,768]{1,0:T(8,128)S(1)}, u32[]{:S(2)}, u32[]{:S(2)}) %collective-permute-start.4) | collective-permute-done | bytes 196640 | tf_op jit(solution)/shard_map/ppermute | solution.py:221
  7.8 0.3 %collective-permute-start.6 = (f32[64,768]{1,0:T(8,128)S(1)}, f32[64,768]{1,0:T(8,128)S(1)}, u32[]{:S(2)}, u32[]{:S(2)}) collective-permute-start(f32[64,768]{1,0:T(8,128)S(1)} %get-tuple-element.28.held), channel_id=1, source_target_pairs={{0,4},{1,5},{2,6},{3,7},{4,0},{5,1},{6,2},{7,3},{8,12},{9,13},{10,... | collective-permute-start | bytes 589832 | tf_op jit(solution)/shard_map/ppermute | solution.py:221
  8.2 0.3 collective-permute-start.5
  8.5 0.9 %collective-permute-done.6.refs_0_.inside = f32[64,768]{1,0:T(8,128)S(1)} collective-permute-done((f32[64,768]{1,0:T(8,128)S(1)}, f32[64,768]{1,0:T(8,128)S(1)}, u32[]{:S(2)}, u32[]{:S(2)}) %collective-permute-start.6) | collective-permute-done | bytes 196640 | tf_op jit(solution)/shard_map/ppermute | solution.py:221
  9.3 0.4 %collective-permute-start.7 = (f32[64,768]{1,0:T(8,128)S(1)}, f32[64,768]{1,0:T(8,128)S(1)}, u32[]{:S(2)}, u32[]{:S(2)}) collective-permute-start(f32[64,768]{1,0:T(8,128)S(1)} %product_32.1), channel_id=1, source_target_pairs={{14,15},{15,11},{11,10},{10,14},{0,4},{1,5},{2,6},{3,7},{4,0},{5,1... | collective-permute-start | bytes 589832 | tf_op jit(solution)/shard_map/ppermute | solution.py:221
  9.7 0.2 collective-permute-start.9
  9.9 0.3 collective-permute-start.10
  10.2 0.6 %collective-permute-done.7.got = f32[64,768]{1,0:T(8,128)S(1)} collective-permute-done((f32[64,768]{1,0:T(8,128)S(1)}, f32[64,768]{1,0:T(8,128)S(1)}, u32[]{:S(2)}, u32[]{:S(2)}) %collective-permute-start.7) | collective-permute-done | bytes 196640 | tf_op jit(solution)/shard_map/ppermute | solution.py:221
  10.9 0.1 solve_3.1
  11.0 0.4 %collective-permute-start.8 = (f32[64,192]{1,0:T(8,128)S(1)}, f32[64,192]{1,0:T(8,128)S(1)}, u32[]{:S(2)}, u32[]{:S(2)}) collective-permute-start(f32[64,192]{1,0:T(8,128)S(1)} %get-tuple-element.30), channel_id=1, source_target_pairs={{0,4},{1,5},{2,6},{3,7},{4,0},{5,1},{6,2},{7,3},{8,12},{9,13},{10,... | collective-permute-start | bytes 147464 | tf_op jit(solution)/shard_map/ppermute | solution.py:221
  11.4 15.7 %collective-permute-start.11 = (f32[64,192]{1,0:T(8,128)S(1)}, f32[64,192]{1,0:T(8,128)S(1)}, u32[]{:S(2)}, u32[]{:S(2)}) collective-permute-start(f32[64,192]{1,0:T(8,128)S(1)} %get-tuple-element.33), channel_id=1, source_target_pairs={{15,3},{3,7},{7,11},{11,15},{0,4},{1,5},{2,6},{4,0},{5,1},{6,2},{8... | collective-permute-start | bytes 147464 | tf_op jit(solution)/shard_map/ppermute | solution.py:221
  27.1 1.3 %collective-permute-done.11.zero = f32[64,192]{1,0:T(8,128)S(1)} collective-permute-done((f32[64,192]{1,0:T(8,128)S(1)}, f32[64,192]{1,0:T(8,128)S(1)}, u32[]{:S(2)}, u32[]{:S(2)}) %collective-permute-start.11) | collective-permute-done | bytes 49184 | tf_op jit(solution)/shard_map/ppermute | solution.py:221
  28.4 1.8 %collective-permute-done.12.one = f32[64,192]{1,0:T(8,128)S(1)} collective-permute-done((f32[64,192]{1,0:T(8,128)S(1)}, f32[64,192]{1,0:T(8,128)S(1)}, u32[]{:S(2)}, u32[]{:S(2)}) %collective-permute-start.12) | collective-permute-done | bytes 49184 | tf_op jit(solution)/shard_map/ppermute | solution.py:221
  30.2 0.6 %copy.4 = f32[1,192,64]{1,2,0:T(8,128)} copy(f32[1,192,64]{1,2,0:T(8,128)S(1)} %bitcast.7) | data formatting | bytes 98304
  (13 shorter events, 0.2 us)
Async XLA Ops:
  1.0 1.8 %collective-permute-start = (f32[64,768]{1,0:T(8,128)S(1)}, f32[64,768]{1,0:T(8,128)S(1)}, u32[]{:S(2)}, u32[]{:S(2)}) collective-permute-start(f32[64,768]{1,0:T(8,128)S(1)} %get-tuple-element.22.held), channel_id=1, source_target_pairs={{0,4},{1,5},{2,6},{3,7},{4,0},{5,1},{6,2},{7,3},{8,12},{9,13},{10,... | collective-permute-start | bytes 589832 | tf_op jit(solution)/shard_map/ppermute | solution.py:221
  2.8 1.5 %collective-permute-start.1 = (f32[64,768]{1,0:T(8,128)S(1)}, f32[64,768]{1,0:T(8,128)S(1)}, u32[]{:S(2)}, u32[]{:S(2)}) collective-permute-start(f32[64,768]{1,0:T(8,128)S(1)} %product_10.1.after), channel_id=1, source_target_pairs={{4,5},{5,1},{1,0},{0,8},{8,12},{12,4},{2,6},{3,7},{6,2},{7,3},{9,1... | collective-permute-start | bytes 589832 | tf_op jit(solution)/shard_map/ppermute | solution.py:221
  4.3 1.5 %collective-permute-start.2 = (f32[64,768]{1,0:T(8,128)S(1)}, f32[64,768]{1,0:T(8,128)S(1)}, u32[]{:S(2)}, u32[]{:S(2)}) collective-permute-start(f32[64,768]{1,0:T(8,128)S(1)} %solve_1.1.held), channel_id=1, source_target_pairs={{5,9},{9,1},{1,5},{0,12},{12,8},{8,13},{13,4},{4,0},{2,6},{3,7},{6... | collective-permute-start | bytes 589832 | tf_op jit(solution)/shard_map/ppermute | solution.py:221
  5.9 1.5 %collective-permute-start.3 = (f32[64,768]{1,0:T(8,128)S(1)}, f32[64,768]{1,0:T(8,128)S(1)}, u32[]{:S(2)}, u32[]{:S(2)}) collective-permute-start(f32[64,768]{1,0:T(8,128)S(1)} %get-tuple-element.26), channel_id=1, source_target_pairs={{9,13},{13,9},{8,10},{10,14},{14,6},{6,2},{2,12},{12,8},{0,4},{1,5... | collective-permute-start | bytes 589832 | tf_op jit(solution)/shard_map/ppermute | solution.py:221
  6.3 1.4 %collective-permute-start.4 = (f32[64,768]{1,0:T(8,128)S(1)}, f32[64,768]{1,0:T(8,128)S(1)}, u32[]{:S(2)}, u32[]{:S(2)}) collective-permute-start(f32[64,768]{1,0:T(8,128)S(1)} %get-tuple-element.27.held), channel_id=1, source_target_pairs={{9,10},{10,14},{14,8},{8,12},{12,13},{13,9},{0,4},{1,5},{2,6},{3,7... | collective-permute-start | bytes 589832 | tf_op jit(solution)/shard_map/ppermute | solution.py:221
  7.8 1.5 %collective-permute-start.6 = (f32[64,768]{1,0:T(8,128)S(1)}, f32[64,768]{1,0:T(8,128)S(1)}, u32[]{:S(2)}, u32[]{:S(2)}) collective-permute-start(f32[64,768]{1,0:T(8,128)S(1)} %get-tuple-element.28.held), channel_id=1, source_target_pairs={{0,4},{1,5},{2,6},{3,7},{4,0},{5,1},{6,2},{7,3},{8,12},{9,13},{10,... | collective-permute-start | bytes 589832 | tf_op jit(solution)/shard_map/ppermute | solution.py:221
  8.2 2.0 %collective-permute-start.5 = (f32[64,768]{1,0:T(8,128)S(1)}, f32[64,768]{1,0:T(8,128)S(1)}, u32[]{:S(2)}, u32[]{:S(2)}) collective-permute-start(f32[64,768]{1,0:T(8,128)S(1)} %product_31.1), channel_id=1, source_target_pairs={{13,15},{15,11},{11,9},{9,13},{0,4},{1,5},{2,6},{3,7},{4,0},{5,1},... | collective-permute-start | bytes 589832 | tf_op jit(solution)/shard_map/ppermute | solution.py:221
  9.3 1.5 %collective-permute-start.7 = (f32[64,768]{1,0:T(8,128)S(1)}, f32[64,768]{1,0:T(8,128)S(1)}, u32[]{:S(2)}, u32[]{:S(2)}) collective-permute-start(f32[64,768]{1,0:T(8,128)S(1)} %product_32.1), channel_id=1, source_target_pairs={{14,15},{15,11},{11,10},{10,14},{0,4},{1,5},{2,6},{3,7},{4,0},{5,1... | collective-permute-start | bytes 589832 | tf_op jit(solution)/shard_map/ppermute | solution.py:221
  9.7 17.4 %collective-permute-start.9 = (f32[64,192]{1,0:T(8,128)S(1)}, f32[64,192]{1,0:T(8,128)S(1)}, u32[]{:S(2)}, u32[]{:S(2)}) collective-permute-start(f32[64,192]{1,0:T(8,128)S(1)} %get-tuple-element.31), channel_id=1, source_target_pairs={{10,2},{2,10},{14,6},{6,14},{0,4},{1,5},{3,7},{4,0},{5,1},{7,3},{8... | collective-permute-start | bytes 147464 | tf_op jit(solution)/shard_map/ppermute | solution.py:221
  9.9 17.1 %collective-permute-start.10 = (f32[64,192]{1,0:T(8,128)S(1)}, f32[64,192]{1,0:T(8,128)S(1)}, u32[]{:S(2)}, u32[]{:S(2)}) collective-permute-start(f32[64,192]{1,0:T(8,128)S(1)} %get-tuple-element.32), channel_id=1, source_target_pairs={{10,6},{6,10},{14,2},{2,14},{0,4},{1,5},{3,7},{4,0},{5,1},{7,3},{8... | collective-permute-start | bytes 147464 | tf_op jit(solution)/shard_map/ppermute | solution.py:221
  11.0 16.1 %collective-permute-start.8 = (f32[64,192]{1,0:T(8,128)S(1)}, f32[64,192]{1,0:T(8,128)S(1)}, u32[]{:S(2)}, u32[]{:S(2)}) collective-permute-start(f32[64,192]{1,0:T(8,128)S(1)} %get-tuple-element.30), channel_id=1, source_target_pairs={{0,4},{1,5},{2,6},{3,7},{4,0},{5,1},{6,2},{7,3},{8,12},{9,13},{10,... | collective-permute-start | bytes 147464 | tf_op jit(solution)/shard_map/ppermute | solution.py:221
  11.4 17.0 %collective-permute-start.11 = (f32[64,192]{1,0:T(8,128)S(1)}, f32[64,192]{1,0:T(8,128)S(1)}, u32[]{:S(2)}, u32[]{:S(2)}) collective-permute-start(f32[64,192]{1,0:T(8,128)S(1)} %get-tuple-element.33), channel_id=1, source_target_pairs={{15,3},{3,7},{7,11},{11,15},{0,4},{1,5},{2,6},{4,0},{5,1},{6,2},{8... | collective-permute-start | bytes 147464 | tf_op jit(solution)/shard_map/ppermute | solution.py:221
  27.1 3.1 %collective-permute-start.12 = (f32[64,192]{1,0:T(8,128)S(1)}, f32[64,192]{1,0:T(8,128)S(1)}, u32[]{:S(2)}, u32[]{:S(2)}) collective-permute-start(f32[64,192]{1,0:T(8,128)S(1)} %get-tuple-element.34), channel_id=1, source_target_pairs={{15,7},{7,3},{3,11},{11,15},{0,4},{1,5},{2,6},{4,0},{5,1},{6,2},{8... | collective-permute-start | bytes 147464 | tf_op jit(solution)/shard_map/ppermute | solution.py:221

commit v3 on v2

v3 whole, which is shorter than its diff:
```python
import functools

import jax
import jax.numpy as jnp
from jax import lax
from jax.experimental import pallas as pl
from jax.experimental.pallas import tpu as pltpu
from jax.sharding import PartitionSpec as P

GRID = ("row", "col")
LOADS = 3
PIECES = 2
FLAT = (((1,), (0,)), ((), ()))
TURNED = (((1,), (1,)), ((), ()))
SIDE = 4


def split(values):
    big = values.astype(jnp.bfloat16)
    return big, (values - big.astype(jnp.float32)).astype(jnp.bfloat16)


def product(columns, big, small, dims):
    count = columns.shape[0]
    high, low = split(columns)
    dot = functools.partial(lax.dot_general, dimension_numbers=dims, preferred_element_type=jnp.float32)
    both = dot(jnp.concatenate([high, low], 0), big)
    return both[:count] + (both[count:] + dot(high, small))


def here(row, col):
    return (lax.axis_index("row") == row) & (lax.axis_index("col") == col)


def call(kernel, name, outs, args, spaces=None, scratch=(), flops=0, size=0):
    spaces = spaces or [pltpu.VMEM] * len(args)
    many = isinstance(outs, list)
    kept = [pltpu.VMEM(out.shape, out.dtype) for out in (outs if many else [outs])]
    args = [pltpu.with_memory_space_constraint(a, s) if s is pltpu.HBM else a for a, s in zip(args, spaces)]
    found = pl.pallas_call(
        kernel,
        out_shape=kept,
        in_specs=[pl.BlockSpec(memory_space=space) for space in spaces],
        out_specs=[pl.BlockSpec(memory_space=pltpu.VMEM)] * len(kept),
        scratch_shapes=scratch,
        compiler_params=pltpu.CompilerParams(vmem_limit_bytes=24 << 20),
        cost_estimate=pl.CostEstimate(flops=flops, bytes_accessed=size, transcendentals=0),
        name=name,
    )(*args)
    return found if many else found[0]


def like(array, dtype=None, shape=None):
    return jax.ShapeDtypeStruct(shape or array.shape, dtype or array.dtype)


def fetch(factor_hbm, pattern_hbm, buffer, links, sems):
    rows = buffer.shape[0] // LOADS
    copies = [pltpu.make_async_copy(pattern_hbm, links, sems.at[LOADS])]
    for k in range(LOADS):
        part = pl.ds(k * rows, rows)
        copies.append(pltpu.make_async_copy(factor_hbm.at[part], buffer.at[part], sems.at[k]))
    for copy in copies:
        copy.start()
    return copies


def turn_block(copies, buffer, links, big_ref, small_ref):
    row, col = lax.axis_index("row"), lax.axis_index("col")
    copies[0].wait()
    used = (row == col) | (links[row, col] == 1)
    rows = buffer.shape[0] // LOADS
    for k in range(LOADS):
        copies[k + 1].wait()
        part = slice(k * rows, (k + 1) * rows)
        big_ref[:, part], small_ref[:, part] = split(jnp.where(used, buffer[part], 0.0).T)


def open_chain(factor_hbm, right_hbm, pattern_hbm, big_ref, small_ref, *rest):
    found, (right, buffer, links, sems) = rest[:PIECES], rest[PIECES:]
    count = found[0].shape[0]

    @pl.when(here(0, 0))
    def _():
        load = pltpu.make_async_copy(right_hbm, right, sems.at[LOADS + 1])
        load.start()
        copies = fetch(factor_hbm, pattern_hbm, buffer, links, sems)
        load.wait()
        rows = buffer.shape[0] // LOADS
        for k in range(LOADS):
            copies[k + 1].wait()
            part = slice(k * rows, (k + 1) * rows)
            answer = product(right[...], *split(buffer[part]), TURNED)
            for n, ref in enumerate(found):
                ref[:, part] = answer[n * count : (n + 1) * count]
        copies[0].wait()

    @pl.when(here(1, 0))
    def _():
        turn_block(fetch(factor_hbm, pattern_hbm, buffer, links, sems), buffer, links, big_ref, small_ref)

    @pl.when(jnp.logical_not(here(0, 0)))
    def _():
        for ref in found:
            ref[...] = jnp.zeros_like(ref)


def load_block(factor_hbm, right_hbm, pattern_hbm, *rest):
    big_ref, small_ref, *rest = rest[PIECES:]
    right, (buffer, links, sems) = rest[:PIECES], rest[PIECES:]
    count = right[0].shape[0]
    row, col = lax.axis_index("row"), lax.axis_index("col")

    @pl.when((row >= col) & jnp.logical_not(here(0, 0) | here(1, 0)))
    def _():
        loads = [
            pltpu.make_async_copy(right_hbm.at[pl.ds(n * count, count)], ref, sems.at[LOADS + 1 + n])
            for n, ref in enumerate(right)
        ]
        for load in loads:
            load.start()
        turn_block(fetch(factor_hbm, pattern_hbm, buffer, links, sems), buffer, links, big_ref, small_ref)
        for load in loads:
            load.wait()


def advance(rules, plain, big, small, held, *refs):
    sources, out = refs[:-1], refs[-1]
    out[...] = held[...]
    for spot in sorted({*rules, *plain}):

        @pl.when(here(*spot))
        def _(spot=spot):
            given = [source[...] for source in sources]
            terms = [product(rules[spot](*given), big[...], small[...], FLAT)] if spot in rules else []
            terms += [plain[spot](*given)] if spot in plain else []
            out[...] = sum(terms[1:], terms[0])


def share_of(ref, row):
    wide = ref.shape[1] // SIDE
    return ref[:, row * wide : (row + 1) * wide]


def step_one(big, small, held, right, second, out, side):
    out[...] = held[...]
    side[...] = jnp.zeros_like(side)

    @pl.when(here(1, 1))
    def _():
        out[...] = product(right[...] - second[...], big[...], small[...], FLAT)

    @pl.when(here(2, 0))
    def _():
        out[...] = second[...]
        side[...] = product(second[...], big[...], small[...], FLAT)


def join(held, side, out):
    out[...] = held[...]

    @pl.when(here(2, 1))
    def _():
        out[...] += side[...]


def pass_two(big, small, held, right, got, after, out):
    out[...] = held[...]

    @pl.when(here(2, 2))
    def _():
        out[...] = product(right[...] - got[...], big[...], small[...], FLAT)


def hand_over(*refs):
    solved, (across, zero, one) = refs[:PIECES], refs[PIECES:]
    count = solved[0].shape[0]
    row = lax.axis_index("row")
    for n, ref in enumerate(solved):
        part = slice(n * count, (n + 1) * count)
        for k in range(SIDE):

            @pl.when(row == (k ^ 1))
            def _(ref=ref, part=part, k=k):
                across[part] = share_of(ref, k)

        zero[part] = share_of(ref, 0)
        one[part] = share_of(ref, 1)


def hand_middle(*refs):
    held, inside, out = refs[:PIECES], refs[PIECES : 2 * PIECES], refs[-1]
    count = held[0].shape[0]
    for n in range(PIECES):
        part = slice(n * count, (n + 1) * count)
        out[part] = share_of(held[n], 0)

        @pl.when(here(3, 2))
        def _(n=n, part=part):
            out[part] = share_of(inside[n], 1)


def close_chain(piece, big, small, held, right, middle, got, out):
    out[...] = held[...]

    @pl.when(here(3, 3))
    def _():
        count = out.shape[0]
        columns = right[...] - middle[piece * count : (piece + 1) * count] - got[...]
        out[...] = product(columns, big[...], small[...], FLAT)


def beside_sum(big, small, *refs):
    beside, fourth, out = refs[:PIECES], refs[PIECES : 2 * PIECES], refs[-1]
    count = beside[0].shape[0]

    @pl.when(here(3, 1))
    def _():
        columns = jnp.concatenate([ref[...] for ref in beside], 0)
        answer = product(columns, big[...], small[...], FLAT)
        for n, ref in enumerate(fourth):
            part = slice(n * count, (n + 1) * count)
            out[part] = answer[part] + ref[...]

    @pl.when(jnp.logical_not(here(3, 1)))
    def _():
        out[...] = jnp.zeros_like(out)


def give(*refs):
    *lists, across, above, zero, one, out = refs
    count = out.shape[0] // PIECES
    share = {
        (0, 1): across, (2, 3): across,
        (0, 2): above, (1, 2): above, (0, 3): zero, (1, 3): one,
    }
    for (row, col), ref in share.items():

        @pl.when(here(row, col))
        def _(ref=ref):
            out[...] = ref[...]

    for n in range(PIECES):
        held, first, second, third, beside, inside = lists[n::PIECES]
        whole = {
            (0, 0): held, (1, 0): first, (2, 0): second, (3, 0): third,
            (1, 1): held, (2, 1): third, (3, 1): beside,
            (2, 2): held, (3, 2): inside, (3, 3): held,
        }
        for (row, col), ref in whole.items():

            @pl.when(here(row, col))
            def _(row=row, ref=ref, part=slice(n * count, (n + 1) * count)):
                out[part] = share_of(ref, row)


def route(*cycles):
    target = {}
    for cycle in cycles:
        for spot, source in enumerate(cycle):
            target[source] = cycle[(spot + 1) % len(cycle)]
    for row in range(SIDE):
        for col in range(SIDE):
            target.setdefault((row, col), (row ^ 1, col))
    assert sorted(target) == sorted(target.values())
    return [(a * SIDE + b, c * SIDE + d) for (a, b), (c, d) in target.items()]


ROUTES = {
    "solved_0": route(),
    "product_10": route([(1, 0), (1, 1), (0, 1), (0, 0), (2, 0), (3, 0)]),
    "solved_1": route([(1, 1), (2, 1), (3, 1), (0, 1)]),
    "product_20": route([(2, 0), (2, 1), (3, 1), (3, 0)]),
    "product_21": route([(2, 1), (2, 2), (3, 2), (1, 2), (0, 2), (2, 0), (3, 0), (3, 1)]),
    "beside": route(),
    "product_31": route([(3, 1), (3, 3), (2, 3), (2, 1)]),
    "solved_2": route(),
    "product_32": route([(3, 2), (3, 3), (2, 3), (2, 2)]),
    "share_2": route([(2, 2), (0, 2)], [(3, 2), (1, 2)]),
    "share_3": route(),
    "share_03": route([(3, 3), (0, 3), (1, 3), (2, 3)]),
    "share_13": route([(3, 3), (1, 3), (0, 3), (2, 3)]),
}


def send(name, array):
    with jax.named_scope(name):
        return lax.ppermute(array, GRID, ROUTES[name])


def chain(factor, rhs, pattern):
    block = factor[0, 0]
    order = block.shape[0]
    turned = rhs[0].T
    count = turned.shape[0] // PIECES
    half, vector = like(block, jnp.bfloat16), like(turned, shape=(count, order))
    work = 6 * order * order * count
    weight = dict(flops=work, size=4 * order * order)
    buffers = [pltpu.VMEM(block.shape, block.dtype), pltpu.SMEM(pattern.shape, pattern.dtype)]

    def move(name, rules, *lists, shared):
        return [
            call(functools.partial(advance, rules, {}), name, vector, (*shared, *args), **weight)
            for args in zip(*lists)
        ]

    def sends(name, arrays):
        return [send(name, array) for array in arrays]

    inputs = (block, turned, pattern)
    semaphores = pltpu.SemaphoreType.DMA((LOADS + 1 + PIECES,))
    big, small, *held = call(
        open_chain, "open_chain", [half, half] + [vector] * PIECES, inputs, [pltpu.HBM] * 3,
        [pltpu.VMEM(turned.shape, turned.dtype), *buffers, semaphores], **weight,
    )
    first = sends("solved_0", held)
    carried = move("product_10", {(1, 0): lambda first: first}, held, first, shared=(big, small))
    second = sends("product_10", carried)
    big, small, *right = call(
        load_block, "load_block", [half, half] + [vector] * PIECES, (*inputs, *carried), [pltpu.HBM] * 3 + [pltpu.VMEM] * PIECES,
        [*buffers, semaphores], **weight,
    )
    shared = (big, small)
    pairs = [
        call(step_one, "solve_1", [vector, vector], (*shared, *args), **weight) for args in zip(held, right, second)
    ]
    held, side = zip(*pairs)
    third, side = sends("solved_1", held), sends("product_20", side)
    carried = move("product_21", {(2, 1): lambda got: got, (3, 0): lambda got: got}, held, third, shared=shared)
    carried = [call(join, "join_2", vector, args, flops=1, size=1) for args in zip(carried, side)]
    fourth, beside = sends("product_21", carried), sends("beside", third)
    aside = call(beside_sum, "product_31", like(turned), (*shared, *beside, *fourth), **weight)
    middle = send("product_31", aside)
    after = fourth[0]
    solved, inside, last = [], [], []
    for n in range(PIECES):
        solved.append(call(pass_two, "solve_2", vector, (*shared, held[n], right[n], fourth[n], after), **weight))
        inside.append(send("solved_2", solved[n]))
        (after,) = move("product_32", {(3, 2): lambda got: got}, carried[n : n + 1], inside[n:], shared=shared)
        last.append(send("product_32", after))
    held = solved
    whole = like(turned, shape=(turned.shape[0], order // SIDE))
    above = send("share_2", call(hand_middle, "share_2", whole, (*held, *inside)))
    held = [
        call(functools.partial(close_chain, n), "solve_3", vector, (*shared, held[n], right[n], middle, last[n]), **weight)
        for n in range(PIECES)
    ]
    across, zero, one = call(hand_over, "share_3", [whole] * 3, held)
    across, zero, one = send("share_3", across), send("share_03", zero), send("share_13", one)
    lists = (held, first, second, third, beside, inside)
    given = call(give, "give", whole, [*[a for l in lists for a in l], across, above, zero, one])
    return given.T[None]


def from_root(shard, axis, root):
    mine = lax.axis_index(axis) == root
    return lax.psum(jnp.where(mine, shard, jnp.zeros_like(shard)), axis)


def multiply(factor_tile, columns):
    return jnp.dot(factor_tile, columns, precision=lax.Precision.HIGHEST, preferred_element_type=jnp.float32)


def levels(factor, rhs, pattern):
    block, right = factor[0, 0], rhs[0]
    row, col = lax.axis_index("row"), lax.axis_index("col")
    depth = min(6, lax.axis_size("row"))
    height = jnp.zeros((pattern.shape[0],), jnp.int32)
    for _ in range(depth):
        height = jnp.max(jnp.where(pattern == 1, height[None, :] + 1, 0), axis=1)
    solved = carried = jnp.zeros_like(right)
    times = functools.partial(multiply, block)
    for level in range(depth):
        solve_now = (row == col) & (height[row] == level)
        fresh = lax.cond(solve_now, times, jnp.zeros_like, right - carried)
        arrived = from_root(fresh, "row", col)
        if level < depth - 1:
            apply_now = (pattern[row, col] == 1) & (height[col] == level)
            carried = carried + lax.psum(lax.cond(apply_now, times, jnp.zeros_like, arrived), "col")
        solved = solved + arrived
    share = solved.shape[0] // lax.axis_size("row")
    return lax.dynamic_slice_in_dim(solved, row * share, share, 0)[None]


def solution(mesh):
    in_specs = (P(("grp", "row"), "col", None, None), P(("grp", "row"), None, None), P("grp", None))
    out_specs = P(("grp", "col"), "row", None)
    local = chain if mesh.shape["row"] == mesh.shape["col"] == SIDE else levels
    return jax.shard_map(local, mesh=mesh, in_specs=in_specs, out_specs=out_specs, check_vma=False)
```

time: 31 us -> 28 us (0.903)
  waiting for transfers between devices: 9.08 us -> 7.69 us
  Pallas kernels: 1.31 us -> 0.49 us
  starting transfers between devices: 19.7 us -> 18.9 us
    ppermute x13 -> x21, waiting for transfers between devices: 9.08 us -> 7.69 us  [send(): return lax.ppermute(array, GRID, ROUTES[name])]
    pallas_call x10 -> x20, Pallas kernels: 1.31 us -> 0.49 us  [call(): pl.pallas_call(kernel, out_shape=kept, in_specs=[pl.BlockSpec(memory_spac...]
    ppermute x13 -> x21, starting transfers between devices: 19.7 us -> 18.9 us  [send(): return lax.ppermute(array, GRID, ROUTES[name])]
  transfers between devices with their start and end apart: 13 -> 21, of which waited for: 9 -> 12; matrix products, arithmetic and copies ran while one was open for 0% -> 0% of each run, Pallas kernels for 1% -> 2%
where the time goes in v3:
time: 28 us; the launch traced here: 27.9 us
  starting transfers between devices  18.9 us (67%)
  waiting for transfers between devices  7.69 us (27%)
  local copies, waits for them, and re-layouts  0.63 us (2%)
  Pallas kernels  0.49 us (2%)
    ppermute x21, starting transfers between devices, send(): return lax.ppermute(array, GRID, ROUTES[name])  18.9 us
    ppermute x21, waiting for transfers between devices, send(): return lax.ppermute(array, GRID, ROUTES[name])  7.69 us
    unnamed x1, local copies, waits for them, and re-layouts  0.63 us
  transfers between devices with their start and end apart: 21, of which 12 were waited for; matrix products, arithmetic and copies ran while one was open for 0% of the time, Pallas kernels for 2%

profile of v3, /device:TPU:29, one launch (start us, length us, event | category | flops | bytes accessed | tf_op | source)
XLA Modules:
  0.0 27.9 jit_solution(9962627156534704267)
XLA Ops:
  0.1 0.7 %collective-permute-start = (f32[32,768]{1,0:T(8,128)S(1)}, f32[32,768]{1,0:T(8,128)S(1)}, u32[]{:S(2)}, u32[]{:S(2)}) collective-permute-start(f32[32,768]{1,0:T(8,128)S(1)} %get-tuple-element.22.held), channel_id=1, source_target_pairs={{0,4},{1,5},{2,6},{3,7},{4,0},{5,1},{6,2},{7,3},{8,12},{9,13},{10,... | collective-permute-start | bytes 294920 | tf_op jit(solution)/shard_map/solved_0/ppermute | solution.py:288
  0.9 0.9 %collective-permute-done.refs_0_.refs_2_ = f32[32,768]{1,0:T(8,128)S(1)} collective-permute-done((f32[32,768]{1,0:T(8,128)S(1)}, f32[32,768]{1,0:T(8,128)S(1)}, u32[]{:S(2)}, u32[]{:S(2)}) %collective-permute-start) | collective-permute-done | bytes 98336 | tf_op jit(solution)/shard_map/solved_0/ppermute | solution.py:288
  1.8 0.4 %collective-permute-start.2 = (f32[32,768]{1,0:T(8,128)S(1)}, f32[32,768]{1,0:T(8,128)S(1)}, u32[]{:S(2)}, u32[]{:S(2)}) collective-permute-start(f32[32,768]{1,0:T(8,128)S(1)} %product_10.2.rest_0_), channel_id=1, source_target_pairs={{4,5},{5,1},{1,0},{0,8},{8,12},{12,4},{2,6},{3,7},{6,2},{7,3},{9,1... | collective-permute-start | bytes 294920 | tf_op jit(solution)/shard_map/product_10/ppermute | solution.py:288
  2.4 0.7 %collective-permute-done.2.second.refs_4_ = f32[32,768]{1,0:T(8,128)S(1)} collective-permute-done((f32[32,768]{1,0:T(8,128)S(1)}, f32[32,768]{1,0:T(8,128)S(1)}, u32[]{:S(2)}, u32[]{:S(2)}) %collective-permute-start.2) | collective-permute-done | bytes 98336 | tf_op jit(solution)/shard_map/product_10/ppermute | solution.py:288
  3.1 0.4 %collective-permute-start.3 = (f32[32,768]{1,0:T(8,128)S(1)}, f32[32,768]{1,0:T(8,128)S(1)}, u32[]{:S(2)}, u32[]{:S(2)}) collective-permute-start(f32[32,768]{1,0:T(8,128)S(1)} %get-tuple-element.27.held), channel_id=1, source_target_pairs={{5,9},{9,13},{13,1},{1,5},{0,4},{2,6},{3,7},{4,0},{6,2},{7,3},{8,1... | collective-permute-start | bytes 294920 | tf_op jit(solution)/shard_map/solved_1/ppermute | solution.py:288
  3.7 0.4 %collective-permute-start.8 = (f32[32,768]{1,0:T(8,128)S(1)}, f32[32,768]{1,0:T(8,128)S(1)}, u32[]{:S(2)}, u32[]{:S(2)}) collective-permute-start(f32[32,768]{1,0:T(8,128)S(1)} %get-tuple-element.30.held), channel_id=1, source_target_pairs={{5,9},{9,13},{13,1},{1,5},{0,4},{2,6},{3,7},{4,0},{6,2},{7,3},{8,1... | collective-permute-start | bytes 294920 | tf_op jit(solution)/shard_map/solved_1/ppermute | solution.py:288
  4.5 0.3 %collective-permute-done.4.side = f32[32,768]{1,0:T(8,128)S(1)} collective-permute-done((f32[32,768]{1,0:T(8,128)S(1)}, f32[32,768]{1,0:T(8,128)S(1)}, u32[]{:S(2)}, u32[]{:S(2)}) %collective-permute-start.4) | collective-permute-done | bytes 98336 | tf_op jit(solution)/shard_map/product_20/ppermute | solution.py:288
  5.1 0.4 %collective-permute-start.6 = (f32[32,768]{1,0:T(8,128)S(1)}, f32[32,768]{1,0:T(8,128)S(1)}, u32[]{:S(2)}, u32[]{:S(2)}) collective-permute-start(f32[32,768]{1,0:T(8,128)S(1)} %collective-permute-done.3.refs_0_.refs_6_), channel_id=1, source_target_pairs={{0,4},{1,5},{2,6},{3,7},{4,0},{5,1},{6,2},{7,3},{8,12},{9,13},{10,... | collective-permute-start | bytes 294920 | tf_op jit(solution)/shard_map/beside/ppermute | solution.py:288
  5.6 0.4 %collective-permute-start.11 = (f32[32,768]{1,0:T(8,128)S(1)}, f32[32,768]{1,0:T(8,128)S(1)}, u32[]{:S(2)}, u32[]{:S(2)}) collective-permute-start(f32[32,768]{1,0:T(8,128)S(1)} %join_2.3.held), channel_id=1, source_target_pairs={{9,10},{10,14},{14,6},{6,2},{2,8},{8,12},{12,13},{13,9},{0,4},{1,5... | collective-permute-start | bytes 294920 | tf_op jit(solution)/shard_map/product_21/ppermute | solution.py:288
  6.2 0.2 collective-permute-start.13
  6.4 0.3 %collective-permute-done.9.refs_1_.refs_9_ = f32[32,768]{1,0:T(8,128)S(1)} collective-permute-done((f32[32,768]{1,0:T(8,128)S(1)}, f32[32,768]{1,0:T(8,128)S(1)}, u32[]{:S(2)}, u32[]{:S(2)}) %collective-permute-start.9) | collective-permute-done | bytes 98336 | tf_op jit(solution)/shard_map/beside/ppermute | solution.py:288
  6.7 0.2 collective-permute-done.11.refs_3_.got
  7.0 0.4 %collective-permute-start.12 = (f32[64,768]{1,0:T(8,128)S(1)}, f32[64,768]{1,0:T(8,128)S(1)}, u32[]{:S(2)}, u32[]{:S(2)}) collective-permute-start(f32[64,768]{1,0:T(8,128)S(1)} %product_31.1), channel_id=1, source_target_pairs={{13,15},{15,11},{11,9},{9,13},{0,4},{1,5},{2,6},{3,7},{4,0},{5,1},... | collective-permute-start | bytes 589832 | tf_op jit(solution)/shard_map/product_31/ppermute | solution.py:288
  7.6 0.2 collective-permute-start.15
  7.8 0.4 %collective-permute-start.14 = (f32[32,768]{1,0:T(8,128)S(1)}, f32[32,768]{1,0:T(8,128)S(1)}, u32[]{:S(2)}, u32[]{:S(2)}) collective-permute-start(f32[32,768]{1,0:T(8,128)S(1)} %product_32.2.after), channel_id=1, source_target_pairs={{14,15},{15,11},{11,10},{10,14},{0,4},{1,5},{2,6},{3,7},{4,0},{5,1... | collective-permute-start | bytes 294920 | tf_op jit(solution)/shard_map/product_32/ppermute | solution.py:288
  8.2 0.8 %collective-permute-done.15.refs_0_.refs_3_.refs_11_ = f32[32,768]{1,0:T(8,128)S(1)} collective-permute-done((f32[32,768]{1,0:T(8,128)S(1)}, f32[32,768]{1,0:T(8,128)S(1)}, u32[]{:S(2)}, u32[]{:S(2)}) %collective-permute-start.15) | collective-permute-done | bytes 98336 | tf_op jit(solution)/shard_map/solved_2/ppermute | solution.py:288
  9.0 0.2 collective-permute-start.16
  9.2 0.4 %collective-permute-start.18 = (f32[64,192]{1,0:T(8,128)S(1)}, f32[64,192]{1,0:T(8,128)S(1)}, u32[]{:S(2)}, u32[]{:S(2)}) collective-permute-start(f32[64,192]{1,0:T(8,128)S(1)} %share_2.1), channel_id=1, source_target_pairs={{10,2},{2,10},{14,6},{6,14},{0,4},{1,5},{3,7},{4,0},{5,1},{7,3},{8... | collective-permute-start | bytes 147464 | tf_op jit(solution)/shard_map/share_2/ppermute | solution.py:288
  9.6 0.8 %collective-permute-done.16.got = f32[32,768]{1,0:T(8,128)S(1)} collective-permute-done((f32[32,768]{1,0:T(8,128)S(1)}, f32[32,768]{1,0:T(8,128)S(1)}, u32[]{:S(2)}, u32[]{:S(2)}) %collective-permute-start.16) | collective-permute-done | bytes 98336 | tf_op jit(solution)/shard_map/product_32/ppermute | solution.py:288
  10.6 0.3 %collective-permute-start.17 = (f32[64,192]{1,0:T(8,128)S(1)}, f32[64,192]{1,0:T(8,128)S(1)}, u32[]{:S(2)}, u32[]{:S(2)}) collective-permute-start(f32[64,192]{1,0:T(8,128)S(1)} %get-tuple-element.32), channel_id=1, source_target_pairs={{0,4},{1,5},{2,6},{3,7},{4,0},{5,1},{6,2},{7,3},{8,12},{9,13},{10,... | collective-permute-start | bytes 147464 | tf_op jit(solution)/shard_map/share_3/ppermute | solution.py:288
  10.9 13.2 %collective-permute-start.19 = (f32[64,192]{1,0:T(8,128)S(1)}, f32[64,192]{1,0:T(8,128)S(1)}, u32[]{:S(2)}, u32[]{:S(2)}) collective-permute-start(f32[64,192]{1,0:T(8,128)S(1)} %get-tuple-element.33), channel_id=1, source_target_pairs={{15,3},{3,7},{7,11},{11,15},{0,4},{1,5},{2,6},{4,0},{5,1},{6,2},{8... | collective-permute-start | bytes 147464 | tf_op jit(solution)/shard_map/share_03/ppermute | solution.py:288
  24.1 1.3 %collective-permute-done.19.refs_14_ = f32[64,192]{1,0:T(8,128)S(1)} collective-permute-done((f32[64,192]{1,0:T(8,128)S(1)}, f32[64,192]{1,0:T(8,128)S(1)}, u32[]{:S(2)}, u32[]{:S(2)}) %collective-permute-start.19) | collective-permute-done | bytes 49184 | tf_op jit(solution)/shard_map/share_03/ppermute | solution.py:288
  25.4 1.8 %collective-permute-done.20.refs_15_ = f32[64,192]{1,0:T(8,128)S(1)} collective-permute-done((f32[64,192]{1,0:T(8,128)S(1)}, f32[64,192]{1,0:T(8,128)S(1)}, u32[]{:S(2)}, u32[]{:S(2)}) %collective-permute-start.20) | collective-permute-done | bytes 49184 | tf_op jit(solution)/shard_map/share_13/ppermute | solution.py:288
  27.2 0.6 %copy.4 = f32[1,192,64]{1,2,0:T(8,128)} copy(f32[1,192,64]{1,2,0:T(8,128)S(1)} %bitcast.7) | data formatting | bytes 98304
  (39 shorter events, 2.0 us)
Async XLA Ops:
  0.1 1.7 %collective-permute-start = (f32[32,768]{1,0:T(8,128)S(1)}, f32[32,768]{1,0:T(8,128)S(1)}, u32[]{:S(2)}, u32[]{:S(2)}) collective-permute-start(f32[32,768]{1,0:T(8,128)S(1)} %get-tuple-element.22.held), channel_id=1, source_target_pairs={{0,4},{1,5},{2,6},{3,7},{4,0},{5,1},{6,2},{7,3},{8,12},{9,13},{10,... | collective-permute-start | bytes 294920 | tf_op jit(solution)/shard_map/solved_0/ppermute | solution.py:288
  0.8 1.4 %collective-permute-start.1 = (f32[32,768]{1,0:T(8,128)S(1)}, f32[32,768]{1,0:T(8,128)S(1)}, u32[]{:S(2)}, u32[]{:S(2)}) collective-permute-start(f32[32,768]{1,0:T(8,128)S(1)} %get-tuple-element.23.held), channel_id=1, source_target_pairs={{0,4},{1,5},{2,6},{3,7},{4,0},{5,1},{6,2},{7,3},{8,12},{9,13},{10,... | collective-permute-start | bytes 294920 | tf_op jit(solution)/shard_map/solved_0/ppermute | solution.py:288
  1.8 1.3 %collective-permute-start.2 = (f32[32,768]{1,0:T(8,128)S(1)}, f32[32,768]{1,0:T(8,128)S(1)}, u32[]{:S(2)}, u32[]{:S(2)}) collective-permute-start(f32[32,768]{1,0:T(8,128)S(1)} %product_10.2.rest_0_), channel_id=1, source_target_pairs={{4,5},{5,1},{1,0},{0,8},{8,12},{12,4},{2,6},{3,7},{6,2},{7,3},{9,1... | collective-permute-start | bytes 294920 | tf_op jit(solution)/shard_map/product_10/ppermute | solution.py:288
  2.3 1.4 %collective-permute-start.7 = (f32[32,768]{1,0:T(8,128)S(1)}, f32[32,768]{1,0:T(8,128)S(1)}, u32[]{:S(2)}, u32[]{:S(2)}) collective-permute-start(f32[32,768]{1,0:T(8,128)S(1)} %product_10.3.rest_1_), channel_id=1, source_target_pairs={{4,5},{5,1},{1,0},{0,8},{8,12},{12,4},{2,6},{3,7},{6,2},{7,3},{9,1... | collective-permute-start | bytes 294920 | tf_op jit(solution)/shard_map/product_10/ppermute | solution.py:288
  3.1 1.3 %collective-permute-start.3 = (f32[32,768]{1,0:T(8,128)S(1)}, f32[32,768]{1,0:T(8,128)S(1)}, u32[]{:S(2)}, u32[]{:S(2)}) collective-permute-start(f32[32,768]{1,0:T(8,128)S(1)} %get-tuple-element.27.held), channel_id=1, source_target_pairs={{5,9},{9,13},{13,1},{1,5},{0,4},{2,6},{3,7},{4,0},{6,2},{7,3},{8,1... | collective-permute-start | bytes 294920 | tf_op jit(solution)/shard_map/solved_1/ppermute | solution.py:288
  3.5 1.3 %collective-permute-start.4 = (f32[32,768]{1,0:T(8,128)S(1)}, f32[32,768]{1,0:T(8,128)S(1)}, u32[]{:S(2)}, u32[]{:S(2)}) collective-permute-start(f32[32,768]{1,0:T(8,128)S(1)} %get-tuple-element.28), channel_id=1, source_target_pairs={{8,9},{9,13},{13,12},{12,8},{0,4},{1,5},{2,6},{3,7},{4,0},{5,1},{6... | collective-permute-start | bytes 294920 | tf_op jit(solution)/shard_map/product_20/ppermute | solution.py:288
  3.7 1.7 %collective-permute-start.8 = (f32[32,768]{1,0:T(8,128)S(1)}, f32[32,768]{1,0:T(8,128)S(1)}, u32[]{:S(2)}, u32[]{:S(2)}) collective-permute-start(f32[32,768]{1,0:T(8,128)S(1)} %get-tuple-element.30.held), channel_id=1, source_target_pairs={{5,9},{9,13},{13,1},{1,5},{0,4},{2,6},{3,7},{4,0},{6,2},{7,3},{8,1... | collective-permute-start | bytes 294920 | tf_op jit(solution)/shard_map/solved_1/ppermute | solution.py:288
  4.1 1.5 %collective-permute-start.10 = (f32[32,768]{1,0:T(8,128)S(1)}, f32[32,768]{1,0:T(8,128)S(1)}, u32[]{:S(2)}, u32[]{:S(2)}) collective-permute-start(f32[32,768]{1,0:T(8,128)S(1)} %get-tuple-element.31), channel_id=1, source_target_pairs={{8,9},{9,13},{13,12},{12,8},{0,4},{1,5},{2,6},{3,7},{4,0},{5,1},{6... | collective-permute-start | bytes 294920 | tf_op jit(solution)/shard_map/product_20/ppermute | solution.py:288
  4.9 1.4 %collective-permute-start.5 = (f32[32,768]{1,0:T(8,128)S(1)}, f32[32,768]{1,0:T(8,128)S(1)}, u32[]{:S(2)}, u32[]{:S(2)}) collective-permute-start(f32[32,768]{1,0:T(8,128)S(1)} %join_2.2.held), channel_id=1, source_target_pairs={{9,10},{10,14},{14,6},{6,2},{2,8},{8,12},{12,13},{13,9},{0,4},{1,5... | collective-permute-start | bytes 294920 | tf_op jit(solution)/shard_map/product_21/ppermute | solution.py:288
  5.1 1.4 %collective-permute-start.6 = (f32[32,768]{1,0:T(8,128)S(1)}, f32[32,768]{1,0:T(8,128)S(1)}, u32[]{:S(2)}, u32[]{:S(2)}) collective-permute-start(f32[32,768]{1,0:T(8,128)S(1)} %collective-permute-done.3.refs_0_.refs_6_), channel_id=1, source_target_pairs={{0,4},{1,5},{2,6},{3,7},{4,0},{5,1},{6,2},{7,3},{8,12},{9,13},{10,... | collective-permute-start | bytes 294920 | tf_op jit(solution)/shard_map/beside/ppermute | solution.py:288
  5.4 1.3 %collective-permute-start.9 = (f32[32,768]{1,0:T(8,128)S(1)}, f32[32,768]{1,0:T(8,128)S(1)}, u32[]{:S(2)}, u32[]{:S(2)}) collective-permute-start(f32[32,768]{1,0:T(8,128)S(1)} %collective-permute-done.8.refs_0_.refs_7_), channel_id=1, source_target_pairs={{0,4},{1,5},{2,6},{3,7},{4,0},{5,1},{6,2},{7,3},{8,12},{9,13},{10,... | collective-permute-start | bytes 294920 | tf_op jit(solution)/shard_map/beside/ppermute | solution.py:288
  5.6 1.4 %collective-permute-start.11 = (f32[32,768]{1,0:T(8,128)S(1)}, f32[32,768]{1,0:T(8,128)S(1)}, u32[]{:S(2)}, u32[]{:S(2)}) collective-permute-start(f32[32,768]{1,0:T(8,128)S(1)} %join_2.3.held), channel_id=1, source_target_pairs={{9,10},{10,14},{14,6},{6,2},{2,8},{8,12},{12,13},{13,9},{0,4},{1,5... | collective-permute-start | bytes 294920 | tf_op jit(solution)/shard_map/product_21/ppermute | solution.py:288
  6.2 1.4 %collective-permute-start.13 = (f32[32,768]{1,0:T(8,128)S(1)}, f32[32,768]{1,0:T(8,128)S(1)}, u32[]{:S(2)}, u32[]{:S(2)}) collective-permute-start(f32[32,768]{1,0:T(8,128)S(1)} %solve_2.2.held.refs_0_), channel_id=1, source_target_pairs={{0,4},{1,5},{2,6},{3,7},{4,0},{5,1},{6,2},{7,3},{8,12},{9,13},{10,... | collective-permute-start | bytes 294920 | tf_op jit(solution)/shard_map/solved_2/ppermute | solution.py:288
  7.0 2.6 %collective-permute-start.12 = (f32[64,768]{1,0:T(8,128)S(1)}, f32[64,768]{1,0:T(8,128)S(1)}, u32[]{:S(2)}, u32[]{:S(2)}) collective-permute-start(f32[64,768]{1,0:T(8,128)S(1)} %product_31.1), channel_id=1, source_target_pairs={{13,15},{15,11},{11,9},{9,13},{0,4},{1,5},{2,6},{3,7},{4,0},{5,1},... | collective-permute-start | bytes 589832 | tf_op jit(solution)/shard_map/product_31/ppermute | solution.py:288
  7.6 1.4 %collective-permute-start.15 = (f32[32,768]{1,0:T(8,128)S(1)}, f32[32,768]{1,0:T(8,128)S(1)}, u32[]{:S(2)}, u32[]{:S(2)}) collective-permute-start(f32[32,768]{1,0:T(8,128)S(1)} %solve_2.3.held.refs_1_), channel_id=1, source_target_pairs={{0,4},{1,5},{2,6},{3,7},{4,0},{5,1},{6,2},{7,3},{8,12},{9,13},{10,... | collective-permute-start | bytes 294920 | tf_op jit(solution)/shard_map/solved_2/ppermute | solution.py:288
  7.8 1.8 %collective-permute-start.14 = (f32[32,768]{1,0:T(8,128)S(1)}, f32[32,768]{1,0:T(8,128)S(1)}, u32[]{:S(2)}, u32[]{:S(2)}) collective-permute-start(f32[32,768]{1,0:T(8,128)S(1)} %product_32.2.after), channel_id=1, source_target_pairs={{14,15},{15,11},{11,10},{10,14},{0,4},{1,5},{2,6},{3,7},{4,0},{5,1... | collective-permute-start | bytes 294920 | tf_op jit(solution)/shard_map/product_32/ppermute | solution.py:288
  9.0 1.4 %collective-permute-start.16 = (f32[32,768]{1,0:T(8,128)S(1)}, f32[32,768]{1,0:T(8,128)S(1)}, u32[]{:S(2)}, u32[]{:S(2)}) collective-permute-start(f32[32,768]{1,0:T(8,128)S(1)} %product_32.3), channel_id=1, source_target_pairs={{14,15},{15,11},{11,10},{10,14},{0,4},{1,5},{2,6},{3,7},{4,0},{5,1... | collective-permute-start | bytes 294920 | tf_op jit(solution)/shard_map/product_32/ppermute | solution.py:288
  9.2 14.9 %collective-permute-start.18 = (f32[64,192]{1,0:T(8,128)S(1)}, f32[64,192]{1,0:T(8,128)S(1)}, u32[]{:S(2)}, u32[]{:S(2)}) collective-permute-start(f32[64,192]{1,0:T(8,128)S(1)} %share_2.1), channel_id=1, source_target_pairs={{10,2},{2,10},{14,6},{6,14},{0,4},{1,5},{3,7},{4,0},{5,1},{7,3},{8... | collective-permute-start | bytes 147464 | tf_op jit(solution)/shard_map/share_2/ppermute | solution.py:288
  10.6 13.6 %collective-permute-start.17 = (f32[64,192]{1,0:T(8,128)S(1)}, f32[64,192]{1,0:T(8,128)S(1)}, u32[]{:S(2)}, u32[]{:S(2)}) collective-permute-start(f32[64,192]{1,0:T(8,128)S(1)} %get-tuple-element.32), channel_id=1, source_target_pairs={{0,4},{1,5},{2,6},{3,7},{4,0},{5,1},{6,2},{7,3},{8,12},{9,13},{10,... | collective-permute-start | bytes 147464 | tf_op jit(solution)/shard_map/share_3/ppermute | solution.py:288
  10.9 14.6 %collective-permute-start.19 = (f32[64,192]{1,0:T(8,128)S(1)}, f32[64,192]{1,0:T(8,128)S(1)}, u32[]{:S(2)}, u32[]{:S(2)}) collective-permute-start(f32[64,192]{1,0:T(8,128)S(1)} %get-tuple-element.33), channel_id=1, source_target_pairs={{15,3},{3,7},{7,11},{11,15},{0,4},{1,5},{2,6},{4,0},{5,1},{6,2},{8... | collective-permute-start | bytes 147464 | tf_op jit(solution)/shard_map/share_03/ppermute | solution.py:288
  24.1 3.1 %collective-permute-start.20 = (f32[64,192]{1,0:T(8,128)S(1)}, f32[64,192]{1,0:T(8,128)S(1)}, u32[]{:S(2)}, u32[]{:S(2)}) collective-permute-start(f32[64,192]{1,0:T(8,128)S(1)} %get-tuple-element.34), channel_id=1, source_target_pairs={{15,7},{7,3},{3,11},{11,15},{0,4},{1,5},{2,6},{4,0},{5,1},{6,2},{8... | collective-permute-start | bytes 147464 | tf_op jit(solution)/shard_map/share_13/ppermute | solution.py:288

commit v4 on v3

--- a/solution.py
+++ b/solution.py
@@ -173,7 +173,16 @@
 
 
 def hand_over(*refs):
-    solved, (across, zero, one) = refs[:PIECES], refs[PIECES:]
+    solved, (zero, one) = refs[:PIECES], refs[PIECES:]
+    count = solved[0].shape[0]
+    for n, ref in enumerate(solved):
+        part = slice(n * count, (n + 1) * count)
+        zero[part] = share_of(ref, 0)
+        one[part] = share_of(ref, 1)
+
+
+def hand_across(*refs):
+    solved, across = refs[:PIECES], refs[-1]
     count = solved[0].shape[0]
     row = lax.axis_index("row")
     for n, ref in enumerate(solved):
@@ -183,9 +192,6 @@
             @pl.when(row == (k ^ 1))
             def _(ref=ref, part=part, k=k):
                 across[part] = share_of(ref, k)
-
-        zero[part] = share_of(ref, 0)
-        one[part] = share_of(ref, 1)
 
 
 def hand_middle(*refs):
@@ -268,18 +274,18 @@
 
 ROUTES = {
     "solved_0": route(),
-    "product_10": route([(1, 0), (1, 1), (0, 1), (0, 0), (2, 0), (3, 0)]),
-    "solved_1": route([(1, 1), (2, 1), (3, 1), (0, 1)]),
+    "product_10": route([(0, 0), (2, 0), (3, 0), (1, 3), (0, 3), (1, 0), (1, 1), (0, 1)]),
+    "solved_1": route([(0, 1), (1, 1), (2, 1), (3, 1)]),
     "product_20": route([(2, 0), (2, 1), (3, 1), (3, 0)]),
-    "product_21": route([(2, 1), (2, 2), (3, 2), (1, 2), (0, 2), (2, 0), (3, 0), (3, 1)]),
+    "product_21": route([(0, 2), (2, 0), (3, 0), (3, 1), (2, 1), (2, 2), (3, 2), (1, 2)]),
     "beside": route(),
-    "product_31": route([(3, 1), (3, 3), (2, 3), (2, 1)]),
+    "product_31": route([(2, 1), (3, 1), (3, 3), (2, 3)]),
     "solved_2": route(),
-    "product_32": route([(3, 2), (3, 3), (2, 3), (2, 2)]),
-    "share_2": route([(2, 2), (0, 2)], [(3, 2), (1, 2)]),
+    "product_32": route([(0, 2), (2, 2), (3, 2), (3, 3), (2, 3), (1, 3), (0, 3), (1, 2)]),
+    "share_2": route([(0, 2), (2, 2)], [(1, 2), (3, 2)]),
     "share_3": route(),
-    "share_03": route([(3, 3), (0, 3), (1, 3), (2, 3)]),
-    "share_13": route([(3, 3), (1, 3), (0, 3), (2, 3)]),
+    "share_03": route([(0, 3), (1, 3), (2, 3), (3, 3)]),
+    "share_13": route([(0, 3), (2, 3), (3, 3), (1, 3)]),
 }
 
 
@@ -295,7 +301,7 @@
     count = turned.shape[0] // PIECES
     half, vector = like(block, jnp.bfloat16), like(turned, shape=(count, order))
     work = 6 * order * order * count
-    weight = dict(flops=work, size=4 * order * order)
+    weight = dict(flops=1, size=1)
     buffers = [pltpu.VMEM(block.shape, block.dtype), pltpu.SMEM(pattern.shape, pattern.dtype)]
 
     def move(name, rules, *lists, shared):
@@ -345,7 +351,8 @@
         call(functools.partial(close_chain, n), "solve_3", vector, (*shared, held[n], right[n], middle, last[n]), **weight)
         for n in range(PIECES)
     ]
-    across, zero, one = call(hand_over, "share_3", [whole] * 3, held)
+    zero, one = call(hand_over, "share_3", [whole] * 2, held)
+    across = call(hand_across, "across_3", whole, (*held, zero))
     across, zero, one = send("share_3", across), send("share_03", zero), send("share_13", one)
     lists = (held, first, second, third, beside, inside)
     given = call(give, "give", whole, [*[a for l in lists for a in l], across, above, zero, one])

time: 28 us -> 27.1 us (0.968)
  the two profiles are of different devices: /device:TPU:29 before, /device:TPU:30 now
where the time goes in v4:
time: 27.1 us; the launch traced here: 26.9 us
  starting transfers between devices  15.4 us (57%)
  waiting for transfers between devices  10.2 us (38%)
  local copies, waits for them, and re-layouts  0.63 us (2%)
  Pallas kernels  0.54 us (2%)
    ppermute x21, starting transfers between devices, send(): return lax.ppermute(array, GRID, ROUTES[name])  15.4 us
    ppermute x21, waiting for transfers between devices, send(): return lax.ppermute(array, GRID, ROUTES[name])  10.2 us
    unnamed x1, local copies, waits for them, and re-layouts  0.63 us
  transfers between devices with their start and end apart: 21, of which 15 were waited for; matrix products, arithmetic and copies ran while one was open for 0% of the time, Pallas kernels for 2%

profile of v4, /device:TPU:30, one launch (start us, length us, event | category | flops | bytes accessed | tf_op | source)
XLA Modules:
  0.0 26.9 jit_solution(13840409474984576424)
XLA Ops:
  0.2 0.5 %collective-permute-start.1 = (f32[32,768]{1,0:T(8,128)S(1)}, f32[32,768]{1,0:T(8,128)S(1)}, u32[]{:S(2)}, u32[]{:S(2)}) collective-permute-start(f32[32,768]{1,0:T(8,128)S(1)} %get-tuple-element.22.held), channel_id=1, source_target_pairs={{0,4},{1,5},{2,6},{3,7},{4,0},{5,1},{6,2},{7,3},{8,12},{9,13},{10,... | collective-permute-start | bytes 294920 | tf_op jit(solution)/shard_map/solved_0/ppermute | solution.py:294
  0.7 0.8 %collective-permute-done.refs_0_.refs_2_ = f32[32,768]{1,0:T(8,128)S(1)} collective-permute-done((f32[32,768]{1,0:T(8,128)S(1)}, f32[32,768]{1,0:T(8,128)S(1)}, u32[]{:S(2)}, u32[]{:S(2)}) %collective-permute-start) | collective-permute-done | bytes 98336 | tf_op jit(solution)/shard_map/solved_0/ppermute | solution.py:294
  1.6 0.5 %collective-permute-start.7 = (f32[32,768]{1,0:T(8,128)S(1)}, f32[32,768]{1,0:T(8,128)S(1)}, u32[]{:S(2)}, u32[]{:S(2)}) collective-permute-start(f32[32,768]{1,0:T(8,128)S(1)} %product_10.3.rest_1_), channel_id=1, source_target_pairs={{0,8},{8,12},{12,7},{7,3},{3,4},{4,5},{5,1},{1,0},{2,6},{6,2},{9,1... | collective-permute-start | bytes 294920 | tf_op jit(solution)/shard_map/product_10/ppermute | solution.py:294
  2.1 0.7 %collective-permute-done.2.second.refs_4_ = f32[32,768]{1,0:T(8,128)S(1)} collective-permute-done((f32[32,768]{1,0:T(8,128)S(1)}, f32[32,768]{1,0:T(8,128)S(1)}, u32[]{:S(2)}, u32[]{:S(2)}) %collective-permute-start.2) | collective-permute-done | bytes 98336 | tf_op jit(solution)/shard_map/product_10/ppermute | solution.py:294
  2.8 1.6 %collective-permute-start.3 = (f32[32,768]{1,0:T(8,128)S(1)}, f32[32,768]{1,0:T(8,128)S(1)}, u32[]{:S(2)}, u32[]{:S(2)}) collective-permute-start(f32[32,768]{1,0:T(8,128)S(1)} %get-tuple-element.26.held), channel_id=1, source_target_pairs={{1,5},{5,9},{9,13},{13,1},{0,4},{2,6},{3,7},{4,0},{6,2},{7,3},{8,1... | collective-permute-start | bytes 294920 | tf_op jit(solution)/shard_map/solved_1/ppermute | solution.py:294
  4.5 0.5 %collective-permute-start.8 = (f32[32,768]{1,0:T(8,128)S(1)}, f32[32,768]{1,0:T(8,128)S(1)}, u32[]{:S(2)}, u32[]{:S(2)}) collective-permute-start(f32[32,768]{1,0:T(8,128)S(1)} %get-tuple-element.29.held), channel_id=1, source_target_pairs={{1,5},{5,9},{9,13},{13,1},{0,4},{2,6},{3,7},{4,0},{6,2},{7,3},{8,1... | collective-permute-start | bytes 294920 | tf_op jit(solution)/shard_map/solved_1/ppermute | solution.py:294
  5.0 0.3 %collective-permute-done.3.refs_0_.refs_6_ = f32[32,768]{1,0:T(8,128)S(1)} collective-permute-done((f32[32,768]{1,0:T(8,128)S(1)}, f32[32,768]{1,0:T(8,128)S(1)}, u32[]{:S(2)}, u32[]{:S(2)}) %collective-permute-start.3) | collective-permute-done | bytes 98336 | tf_op jit(solution)/shard_map/solved_1/ppermute | solution.py:294
  5.4 0.3 %collective-permute-done.4.side = f32[32,768]{1,0:T(8,128)S(1)} collective-permute-done((f32[32,768]{1,0:T(8,128)S(1)}, f32[32,768]{1,0:T(8,128)S(1)}, u32[]{:S(2)}, u32[]{:S(2)}) %collective-permute-start.4) | collective-permute-done | bytes 98336 | tf_op jit(solution)/shard_map/product_20/ppermute | solution.py:294
  6.0 0.3 %collective-permute-done.10.side = f32[32,768]{1,0:T(8,128)S(1)} collective-permute-done((f32[32,768]{1,0:T(8,128)S(1)}, f32[32,768]{1,0:T(8,128)S(1)}, u32[]{:S(2)}, u32[]{:S(2)}) %collective-permute-start.10) | collective-permute-done | bytes 98336 | tf_op jit(solution)/shard_map/product_20/ppermute | solution.py:294
  6.5 0.4 %collective-permute-start.6 = (f32[32,768]{1,0:T(8,128)S(1)}, f32[32,768]{1,0:T(8,128)S(1)}, u32[]{:S(2)}, u32[]{:S(2)}) collective-permute-start(f32[32,768]{1,0:T(8,128)S(1)} %collective-permute-done.3.refs_0_.refs_6_), channel_id=1, source_target_pairs={{0,4},{1,5},{2,6},{3,7},{4,0},{5,1},{6,2},{7,3},{8,12},{9,13},{10,... | collective-permute-start | bytes 294920 | tf_op jit(solution)/shard_map/beside/ppermute | solution.py:294
  7.1 0.4 %collective-permute-start.13 = (f32[32,768]{1,0:T(8,128)S(1)}, f32[32,768]{1,0:T(8,128)S(1)}, u32[]{:S(2)}, u32[]{:S(2)}) collective-permute-start(f32[32,768]{1,0:T(8,128)S(1)} %solve_2.2.held.refs_0_), channel_id=1, source_target_pairs={{0,4},{1,5},{2,6},{3,7},{4,0},{5,1},{6,2},{7,3},{8,12},{9,13},{10,... | collective-permute-start | bytes 294920 | tf_op jit(solution)/shard_map/solved_2/ppermute | solution.py:294
  7.5 0.3 %collective-permute-done.6.refs_0_.refs_8_ = f32[32,768]{1,0:T(8,128)S(1)} collective-permute-done((f32[32,768]{1,0:T(8,128)S(1)}, f32[32,768]{1,0:T(8,128)S(1)}, u32[]{:S(2)}, u32[]{:S(2)}) %collective-permute-start.6) | collective-permute-done | bytes 98336 | tf_op jit(solution)/shard_map/beside/ppermute | solution.py:294
  7.8 0.4 %collective-permute-done.9.refs_1_.refs_9_ = f32[32,768]{1,0:T(8,128)S(1)} collective-permute-done((f32[32,768]{1,0:T(8,128)S(1)}, f32[32,768]{1,0:T(8,128)S(1)}, u32[]{:S(2)}, u32[]{:S(2)}) %collective-permute-start.9) | collective-permute-done | bytes 98336 | tf_op jit(solution)/shard_map/beside/ppermute | solution.py:294
  8.5 7.6 %collective-permute-start.12 = (f32[64,768]{1,0:T(8,128)S(1)}, f32[64,768]{1,0:T(8,128)S(1)}, u32[]{:S(2)}, u32[]{:S(2)}) collective-permute-start(f32[64,768]{1,0:T(8,128)S(1)} %product_31.1), channel_id=1, source_target_pairs={{9,13},{13,15},{15,11},{11,9},{0,4},{1,5},{2,6},{3,7},{4,0},{5,1},... | collective-permute-start | bytes 589832 | tf_op jit(solution)/shard_map/product_31/ppermute | solution.py:294
  16.3 1.2 %collective-permute-done.15.refs_0_.refs_3_.refs_11_ = f32[32,768]{1,0:T(8,128)S(1)} collective-permute-done((f32[32,768]{1,0:T(8,128)S(1)}, f32[32,768]{1,0:T(8,128)S(1)}, u32[]{:S(2)}, u32[]{:S(2)}) %collective-permute-start.15) | collective-permute-done | bytes 98336 | tf_op jit(solution)/shard_map/solved_2/ppermute | solution.py:294
  17.6 0.5 %collective-permute-start.18 = (f32[64,192]{1,0:T(8,128)S(1)}, f32[64,192]{1,0:T(8,128)S(1)}, u32[]{:S(2)}, u32[]{:S(2)}) collective-permute-start(f32[64,192]{1,0:T(8,128)S(1)} %share_2.1), channel_id=1, source_target_pairs={{2,10},{10,2},{6,14},{14,6},{0,4},{1,5},{3,7},{4,0},{5,1},{7,3},{8... | collective-permute-start | bytes 147464 | tf_op jit(solution)/shard_map/share_2/ppermute | solution.py:294
  18.1 1.2 %collective-permute-done.12.middle = f32[64,768]{1,0:T(8,128)S(1)} collective-permute-done((f32[64,768]{1,0:T(8,128)S(1)}, f32[64,768]{1,0:T(8,128)S(1)}, u32[]{:S(2)}, u32[]{:S(2)}) %collective-permute-start.12) | collective-permute-done | bytes 196640 | tf_op jit(solution)/shard_map/product_31/ppermute | solution.py:294
  19.3 0.5 %collective-permute-done.16.got = f32[32,768]{1,0:T(8,128)S(1)} collective-permute-done((f32[32,768]{1,0:T(8,128)S(1)}, f32[32,768]{1,0:T(8,128)S(1)}, u32[]{:S(2)}, u32[]{:S(2)}) %collective-permute-start.16) | collective-permute-done | bytes 98336 | tf_op jit(solution)/shard_map/product_32/ppermute | solution.py:294
  20.0 1.9 %collective-permute-start.19 = (f32[64,192]{1,0:T(8,128)S(1)}, f32[64,192]{1,0:T(8,128)S(1)}, u32[]{:S(2)}, u32[]{:S(2)}) collective-permute-start(f32[64,192]{1,0:T(8,128)S(1)} %get-tuple-element.31.refs_2_), channel_id=1, source_target_pairs={{3,7},{7,11},{11,15},{15,3},{0,4},{1,5},{2,6},{4,0},{5,1},{6,2},{8... | collective-permute-start | bytes 147464 | tf_op jit(solution)/shard_map/share_03/ppermute | solution.py:294
  22.0 0.4 %collective-permute-start.20 = (f32[64,192]{1,0:T(8,128)S(1)}, f32[64,192]{1,0:T(8,128)S(1)}, u32[]{:S(2)}, u32[]{:S(2)}) collective-permute-start(f32[64,192]{1,0:T(8,128)S(1)} %get-tuple-element.32), channel_id=1, source_target_pairs={{3,11},{11,15},{15,7},{7,3},{0,4},{1,5},{2,6},{4,0},{5,1},{6,2},{8... | collective-permute-start | bytes 147464 | tf_op jit(solution)/shard_map/share_13/ppermute | solution.py:294
  22.5 0.7 %collective-permute-done.17.refs_12_ = f32[64,192]{1,0:T(8,128)S(1)} collective-permute-done((f32[64,192]{1,0:T(8,128)S(1)}, f32[64,192]{1,0:T(8,128)S(1)}, u32[]{:S(2)}, u32[]{:S(2)}) %collective-permute-start.17) | collective-permute-done | bytes 49184 | tf_op jit(solution)/shard_map/share_3/ppermute | solution.py:294
  23.2 0.6 %collective-permute-done.19.refs_14_ = f32[64,192]{1,0:T(8,128)S(1)} collective-permute-done((f32[64,192]{1,0:T(8,128)S(1)}, f32[64,192]{1,0:T(8,128)S(1)}, u32[]{:S(2)}, u32[]{:S(2)}) %collective-permute-start.19) | collective-permute-done | bytes 49184 | tf_op jit(solution)/shard_map/share_03/ppermute | solution.py:294
  23.8 2.5 %collective-permute-done.20.refs_15_ = f32[64,192]{1,0:T(8,128)S(1)} collective-permute-done((f32[64,192]{1,0:T(8,128)S(1)}, f32[64,192]{1,0:T(8,128)S(1)}, u32[]{:S(2)}, u32[]{:S(2)}) %collective-permute-start.20) | collective-permute-done | bytes 49184 | tf_op jit(solution)/shard_map/share_13/ppermute | solution.py:294
  26.3 0.6 %copy.4 = f32[1,192,64]{1,2,0:T(8,128)} copy(f32[1,192,64]{1,2,0:T(8,128)S(1)} %bitcast.7) | data formatting | bytes 98304
  (40 shorter events, 2.1 us)
Async XLA Ops:
  0.1 1.4 %collective-permute-start = (f32[32,768]{1,0:T(8,128)S(1)}, f32[32,768]{1,0:T(8,128)S(1)}, u32[]{:S(2)}, u32[]{:S(2)}) collective-permute-start(f32[32,768]{1,0:T(8,128)S(1)} %get-tuple-element.21.held), channel_id=1, source_target_pairs={{0,4},{1,5},{2,6},{3,7},{4,0},{5,1},{6,2},{7,3},{8,12},{9,13},{10,... | collective-permute-start | bytes 294920 | tf_op jit(solution)/shard_map/solved_0/ppermute | solution.py:294
  0.2 1.5 %collective-permute-start.1 = (f32[32,768]{1,0:T(8,128)S(1)}, f32[32,768]{1,0:T(8,128)S(1)}, u32[]{:S(2)}, u32[]{:S(2)}) collective-permute-start(f32[32,768]{1,0:T(8,128)S(1)} %get-tuple-element.22.held), channel_id=1, source_target_pairs={{0,4},{1,5},{2,6},{3,7},{4,0},{5,1},{6,2},{7,3},{8,12},{9,13},{10,... | collective-permute-start | bytes 294920 | tf_op jit(solution)/shard_map/solved_0/ppermute | solution.py:294
  1.5 1.4 %collective-permute-start.2 = (f32[32,768]{1,0:T(8,128)S(1)}, f32[32,768]{1,0:T(8,128)S(1)}, u32[]{:S(2)}, u32[]{:S(2)}) collective-permute-start(f32[32,768]{1,0:T(8,128)S(1)} %product_10.2.rest_0_), channel_id=1, source_target_pairs={{0,8},{8,12},{12,7},{7,3},{3,4},{4,5},{5,1},{1,0},{2,6},{6,2},{9,1... | collective-permute-start | bytes 294920 | tf_op jit(solution)/shard_map/product_10/ppermute | solution.py:294
  1.6 2.8 %collective-permute-start.7 = (f32[32,768]{1,0:T(8,128)S(1)}, f32[32,768]{1,0:T(8,128)S(1)}, u32[]{:S(2)}, u32[]{:S(2)}) collective-permute-start(f32[32,768]{1,0:T(8,128)S(1)} %product_10.3.rest_1_), channel_id=1, source_target_pairs={{0,8},{8,12},{12,7},{7,3},{3,4},{4,5},{5,1},{1,0},{2,6},{6,2},{9,1... | collective-permute-start | bytes 294920 | tf_op jit(solution)/shard_map/product_10/ppermute | solution.py:294
  2.8 2.5 %collective-permute-start.3 = (f32[32,768]{1,0:T(8,128)S(1)}, f32[32,768]{1,0:T(8,128)S(1)}, u32[]{:S(2)}, u32[]{:S(2)}) collective-permute-start(f32[32,768]{1,0:T(8,128)S(1)} %get-tuple-element.26.held), channel_id=1, source_target_pairs={{1,5},{5,9},{9,13},{13,1},{0,4},{2,6},{3,7},{4,0},{6,2},{7,3},{8,1... | collective-permute-start | bytes 294920 | tf_op jit(solution)/shard_map/solved_1/ppermute | solution.py:294
  4.4 1.3 %collective-permute-start.4 = (f32[32,768]{1,0:T(8,128)S(1)}, f32[32,768]{1,0:T(8,128)S(1)}, u32[]{:S(2)}, u32[]{:S(2)}) collective-permute-start(f32[32,768]{1,0:T(8,128)S(1)} %get-tuple-element.27), channel_id=1, source_target_pairs={{8,9},{9,13},{13,12},{12,8},{0,4},{1,5},{2,6},{3,7},{4,0},{5,1},{6... | collective-permute-start | bytes 294920 | tf_op jit(solution)/shard_map/product_20/ppermute | solution.py:294
  4.5 1.4 %collective-permute-start.8 = (f32[32,768]{1,0:T(8,128)S(1)}, f32[32,768]{1,0:T(8,128)S(1)}, u32[]{:S(2)}, u32[]{:S(2)}) collective-permute-start(f32[32,768]{1,0:T(8,128)S(1)} %get-tuple-element.29.held), channel_id=1, source_target_pairs={{1,5},{5,9},{9,13},{13,1},{0,4},{2,6},{3,7},{4,0},{6,2},{7,3},{8,1... | collective-permute-start | bytes 294920 | tf_op jit(solution)/shard_map/solved_1/ppermute | solution.py:294
  5.0 1.3 %collective-permute-start.10 = (f32[32,768]{1,0:T(8,128)S(1)}, f32[32,768]{1,0:T(8,128)S(1)}, u32[]{:S(2)}, u32[]{:S(2)}) collective-permute-start(f32[32,768]{1,0:T(8,128)S(1)} %get-tuple-element.30), channel_id=1, source_target_pairs={{8,9},{9,13},{13,12},{12,8},{0,4},{1,5},{2,6},{3,7},{4,0},{5,1},{6... | collective-permute-start | bytes 294920 | tf_op jit(solution)/shard_map/product_20/ppermute | solution.py:294
  5.7 1.4 %collective-permute-start.5 = (f32[32,768]{1,0:T(8,128)S(1)}, f32[32,768]{1,0:T(8,128)S(1)}, u32[]{:S(2)}, u32[]{:S(2)}) collective-permute-start(f32[32,768]{1,0:T(8,128)S(1)} %join_2.2.held), channel_id=1, source_target_pairs={{2,8},{8,12},{12,13},{13,9},{9,10},{10,14},{14,6},{6,2},{0,4},{1,5... | collective-permute-start | bytes 294920 | tf_op jit(solution)/shard_map/product_21/ppermute | solution.py:294
  6.3 1.9 %collective-permute-start.11 = (f32[32,768]{1,0:T(8,128)S(1)}, f32[32,768]{1,0:T(8,128)S(1)}, u32[]{:S(2)}, u32[]{:S(2)}) collective-permute-start(f32[32,768]{1,0:T(8,128)S(1)} %join_2.3.held), channel_id=1, source_target_pairs={{2,8},{8,12},{12,13},{13,9},{9,10},{10,14},{14,6},{6,2},{0,4},{1,5... | collective-permute-start | bytes 294920 | tf_op jit(solution)/shard_map/product_21/ppermute | solution.py:294
  6.5 1.3 %collective-permute-start.6 = (f32[32,768]{1,0:T(8,128)S(1)}, f32[32,768]{1,0:T(8,128)S(1)}, u32[]{:S(2)}, u32[]{:S(2)}) collective-permute-start(f32[32,768]{1,0:T(8,128)S(1)} %collective-permute-done.3.refs_0_.refs_6_), channel_id=1, source_target_pairs={{0,4},{1,5},{2,6},{3,7},{4,0},{5,1},{6,2},{7,3},{8,12},{9,13},{10,... | collective-permute-start | bytes 294920 | tf_op jit(solution)/shard_map/beside/ppermute | solution.py:294
  6.9 1.3 %collective-permute-start.9 = (f32[32,768]{1,0:T(8,128)S(1)}, f32[32,768]{1,0:T(8,128)S(1)}, u32[]{:S(2)}, u32[]{:S(2)}) collective-permute-start(f32[32,768]{1,0:T(8,128)S(1)} %collective-permute-done.8.refs_0_.refs_7_), channel_id=1, source_target_pairs={{0,4},{1,5},{2,6},{3,7},{4,0},{5,1},{6,2},{7,3},{8,12},{9,13},{10,... | collective-permute-start | bytes 294920 | tf_op jit(solution)/shard_map/beside/ppermute | solution.py:294
  7.1 1.4 %collective-permute-start.13 = (f32[32,768]{1,0:T(8,128)S(1)}, f32[32,768]{1,0:T(8,128)S(1)}, u32[]{:S(2)}, u32[]{:S(2)}) collective-permute-start(f32[32,768]{1,0:T(8,128)S(1)} %solve_2.2.held.refs_0_), channel_id=1, source_target_pairs={{0,4},{1,5},{2,6},{3,7},{4,0},{5,1},{6,2},{7,3},{8,12},{9,13},{10,... | collective-permute-start | bytes 294920 | tf_op jit(solution)/shard_map/solved_2/ppermute | solution.py:294
  8.5 10.8 %collective-permute-start.12 = (f32[64,768]{1,0:T(8,128)S(1)}, f32[64,768]{1,0:T(8,128)S(1)}, u32[]{:S(2)}, u32[]{:S(2)}) collective-permute-start(f32[64,768]{1,0:T(8,128)S(1)} %product_31.1), channel_id=1, source_target_pairs={{9,13},{13,15},{15,11},{11,9},{0,4},{1,5},{2,6},{3,7},{4,0},{5,1},... | collective-permute-start | bytes 589832 | tf_op jit(solution)/shard_map/product_31/ppermute | solution.py:294
  16.1 1.4 %collective-permute-start.15 = (f32[32,768]{1,0:T(8,128)S(1)}, f32[32,768]{1,0:T(8,128)S(1)}, u32[]{:S(2)}, u32[]{:S(2)}) collective-permute-start(f32[32,768]{1,0:T(8,128)S(1)} %solve_2.3.held.refs_1_), channel_id=1, source_target_pairs={{0,4},{1,5},{2,6},{3,7},{4,0},{5,1},{6,2},{7,3},{8,12},{9,13},{10,... | collective-permute-start | bytes 294920 | tf_op jit(solution)/shard_map/solved_2/ppermute | solution.py:294
  16.2 3.1 %collective-permute-start.14 = (f32[32,768]{1,0:T(8,128)S(1)}, f32[32,768]{1,0:T(8,128)S(1)}, u32[]{:S(2)}, u32[]{:S(2)}) collective-permute-start(f32[32,768]{1,0:T(8,128)S(1)} %product_32.2.after), channel_id=1, source_target_pairs={{2,10},{10,14},{14,15},{15,11},{11,7},{7,3},{3,6},{6,2},{0,4},{1,5... | collective-permute-start | bytes 294920 | tf_op jit(solution)/shard_map/product_32/ppermute | solution.py:294
  17.5 2.3 %collective-permute-start.16 = (f32[32,768]{1,0:T(8,128)S(1)}, f32[32,768]{1,0:T(8,128)S(1)}, u32[]{:S(2)}, u32[]{:S(2)}) collective-permute-start(f32[32,768]{1,0:T(8,128)S(1)} %product_32.3), channel_id=1, source_target_pairs={{2,10},{10,14},{14,15},{15,11},{11,7},{7,3},{3,6},{6,2},{0,4},{1,5... | collective-permute-start | bytes 294920 | tf_op jit(solution)/shard_map/product_32/ppermute | solution.py:294
  17.6 4.9 %collective-permute-start.18 = (f32[64,192]{1,0:T(8,128)S(1)}, f32[64,192]{1,0:T(8,128)S(1)}, u32[]{:S(2)}, u32[]{:S(2)}) collective-permute-start(f32[64,192]{1,0:T(8,128)S(1)} %share_2.1), channel_id=1, source_target_pairs={{2,10},{10,2},{6,14},{14,6},{0,4},{1,5},{3,7},{4,0},{5,1},{7,3},{8... | collective-permute-start | bytes 147464 | tf_op jit(solution)/shard_map/share_2/ppermute | solution.py:294
  20.0 3.7 %collective-permute-start.19 = (f32[64,192]{1,0:T(8,128)S(1)}, f32[64,192]{1,0:T(8,128)S(1)}, u32[]{:S(2)}, u32[]{:S(2)}) collective-permute-start(f32[64,192]{1,0:T(8,128)S(1)} %get-tuple-element.31.refs_2_), channel_id=1, source_target_pairs={{3,7},{7,11},{11,15},{15,3},{0,4},{1,5},{2,6},{4,0},{5,1},{6,2},{8... | collective-permute-start | bytes 147464 | tf_op jit(solution)/shard_map/share_03/ppermute | solution.py:294
  22.0 1.3 %collective-permute-start.17 = (f32[64,192]{1,0:T(8,128)S(1)}, f32[64,192]{1,0:T(8,128)S(1)}, u32[]{:S(2)}, u32[]{:S(2)}) collective-permute-start(f32[64,192]{1,0:T(8,128)S(1)} %across_3.1), channel_id=1, source_target_pairs={{0,4},{1,5},{2,6},{3,7},{4,0},{5,1},{6,2},{7,3},{8,12},{9,13},{10,... | collective-permute-start | bytes 147464 | tf_op jit(solution)/shard_map/share_3/ppermute | solution.py:294
  22.0 4.3 %collective-permute-start.20 = (f32[64,192]{1,0:T(8,128)S(1)}, f32[64,192]{1,0:T(8,128)S(1)}, u32[]{:S(2)}, u32[]{:S(2)}) collective-permute-start(f32[64,192]{1,0:T(8,128)S(1)} %get-tuple-element.32), channel_id=1, source_target_pairs={{3,11},{11,15},{15,7},{7,3},{0,4},{1,5},{2,6},{4,0},{5,1},{6,2},{8... | collective-permute-start | bytes 147464 | tf_op jit(solution)/shard_map/share_13/ppermute | solution.py:294

commit v5 on v4

--- a/solution.py
+++ b/solution.py
@@ -8,7 +8,7 @@
 from jax.sharding import PartitionSpec as P
 
 GRID = ("row", "col")
-LOADS = 3
+LOADS = 2
 PIECES = 2
 FLAT = (((1,), (0,)), ((), ()))
 TURNED = (((1,), (1,)), ((), ()))
@@ -274,7 +274,7 @@
 
 ROUTES = {
     "solved_0": route(),
-    "product_10": route([(0, 0), (2, 0), (3, 0), (1, 3), (0, 3), (1, 0), (1, 1), (0, 1)]),
+    "product_10": route([(0, 0), (2, 0), (3, 0), (3, 2), (2, 2), (1, 0), (1, 1), (0, 1)]),
     "solved_1": route([(0, 1), (1, 1), (2, 1), (3, 1)]),
     "product_20": route([(2, 0), (2, 1), (3, 1), (3, 0)]),
     "product_21": route([(0, 2), (2, 0), (3, 0), (3, 1), (2, 1), (2, 2), (3, 2), (1, 2)]),

time: 27.1 us -> 26.9 us (level)
  no operation moved by 1% of the time
where the time goes in v5:
time: 26.9 us; the launch traced here: 26.7 us
  starting transfers between devices  15.2 us (57%)
  waiting for transfers between devices  10.2 us (38%)
  local copies, waits for them, and re-layouts  0.63 us (2%)
  Pallas kernels  0.52 us (2%)
    ppermute x21, starting transfers between devices, send(): return lax.ppermute(array, GRID, ROUTES[name])  15.2 us
    ppermute x21, waiting for transfers between devices, send(): return lax.ppermute(array, GRID, ROUTES[name])  10.2 us
    unnamed x1, local copies, waits for them, and re-layouts  0.63 us
  transfers between devices with their start and end apart: 21, of which 15 were waited for; matrix products, arithmetic and copies ran while one was open for 0% of the time, Pallas kernels for 2%

profile of v5, /device:TPU:30, one launch (start us, length us, event | category | flops | bytes accessed | tf_op | source)
XLA Modules:
  0.0 26.7 jit_solution(612512391582149673)
XLA Ops:
  0.1 0.5 %collective-permute-start.1 = (f32[32,768]{1,0:T(8,128)S(1)}, f32[32,768]{1,0:T(8,128)S(1)}, u32[]{:S(2)}, u32[]{:S(2)}) collective-permute-start(f32[32,768]{1,0:T(8,128)S(1)} %get-tuple-element.22.held), channel_id=1, source_target_pairs={{0,4},{1,5},{2,6},{3,7},{4,0},{5,1},{6,2},{7,3},{8,12},{9,13},{10,... | collective-permute-start | bytes 294920 | tf_op jit(solution)/shard_map/solved_0/ppermute | solution.py:294
  0.6 0.8 %collective-permute-done.refs_0_.refs_2_ = f32[32,768]{1,0:T(8,128)S(1)} collective-permute-done((f32[32,768]{1,0:T(8,128)S(1)}, f32[32,768]{1,0:T(8,128)S(1)}, u32[]{:S(2)}, u32[]{:S(2)}) %collective-permute-start) | collective-permute-done | bytes 98336 | tf_op jit(solution)/shard_map/solved_0/ppermute | solution.py:294
  1.6 0.5 %collective-permute-start.7 = (f32[32,768]{1,0:T(8,128)S(1)}, f32[32,768]{1,0:T(8,128)S(1)}, u32[]{:S(2)}, u32[]{:S(2)}) collective-permute-start(f32[32,768]{1,0:T(8,128)S(1)} %product_10.3.rest_1_), channel_id=1, source_target_pairs={{0,8},{8,12},{12,14},{14,10},{10,4},{4,5},{5,1},{1,0},{2,6},{3,7},... | collective-permute-start | bytes 294920 | tf_op jit(solution)/shard_map/product_10/ppermute | solution.py:294
  2.1 0.7 %collective-permute-done.2.second.refs_4_ = f32[32,768]{1,0:T(8,128)S(1)} collective-permute-done((f32[32,768]{1,0:T(8,128)S(1)}, f32[32,768]{1,0:T(8,128)S(1)}, u32[]{:S(2)}, u32[]{:S(2)}) %collective-permute-start.2) | collective-permute-done | bytes 98336 | tf_op jit(solution)/shard_map/product_10/ppermute | solution.py:294
  2.8 1.6 %collective-permute-start.3 = (f32[32,768]{1,0:T(8,128)S(1)}, f32[32,768]{1,0:T(8,128)S(1)}, u32[]{:S(2)}, u32[]{:S(2)}) collective-permute-start(f32[32,768]{1,0:T(8,128)S(1)} %get-tuple-element.26.held), channel_id=1, source_target_pairs={{1,5},{5,9},{9,13},{13,1},{0,4},{2,6},{3,7},{4,0},{6,2},{7,3},{8,1... | collective-permute-start | bytes 294920 | tf_op jit(solution)/shard_map/solved_1/ppermute | solution.py:294
  4.5 0.5 %collective-permute-start.8 = (f32[32,768]{1,0:T(8,128)S(1)}, f32[32,768]{1,0:T(8,128)S(1)}, u32[]{:S(2)}, u32[]{:S(2)}) collective-permute-start(f32[32,768]{1,0:T(8,128)S(1)} %get-tuple-element.29.held), channel_id=1, source_target_pairs={{1,5},{5,9},{9,13},{13,1},{0,4},{2,6},{3,7},{4,0},{6,2},{7,3},{8,1... | collective-permute-start | bytes 294920 | tf_op jit(solution)/shard_map/solved_1/ppermute | solution.py:294
  5.1 0.3 %collective-permute-done.3.refs_0_.refs_6_ = f32[32,768]{1,0:T(8,128)S(1)} collective-permute-done((f32[32,768]{1,0:T(8,128)S(1)}, f32[32,768]{1,0:T(8,128)S(1)}, u32[]{:S(2)}, u32[]{:S(2)}) %collective-permute-start.3) | collective-permute-done | bytes 98336 | tf_op jit(solution)/shard_map/solved_1/ppermute | solution.py:294
  5.4 0.3 %collective-permute-done.4.side = f32[32,768]{1,0:T(8,128)S(1)} collective-permute-done((f32[32,768]{1,0:T(8,128)S(1)}, f32[32,768]{1,0:T(8,128)S(1)}, u32[]{:S(2)}, u32[]{:S(2)}) %collective-permute-start.4) | collective-permute-done | bytes 98336 | tf_op jit(solution)/shard_map/product_20/ppermute | solution.py:294
  6.0 0.3 %collective-permute-done.10.side = f32[32,768]{1,0:T(8,128)S(1)} collective-permute-done((f32[32,768]{1,0:T(8,128)S(1)}, f32[32,768]{1,0:T(8,128)S(1)}, u32[]{:S(2)}, u32[]{:S(2)}) %collective-permute-start.10) | collective-permute-done | bytes 98336 | tf_op jit(solution)/shard_map/product_20/ppermute | solution.py:294
  6.6 0.4 %collective-permute-start.6 = (f32[32,768]{1,0:T(8,128)S(1)}, f32[32,768]{1,0:T(8,128)S(1)}, u32[]{:S(2)}, u32[]{:S(2)}) collective-permute-start(f32[32,768]{1,0:T(8,128)S(1)} %collective-permute-done.3.refs_0_.refs_6_), channel_id=1, source_target_pairs={{0,4},{1,5},{2,6},{3,7},{4,0},{5,1},{6,2},{7,3},{8,12},{9,13},{10,... | collective-permute-start | bytes 294920 | tf_op jit(solution)/shard_map/beside/ppermute | solution.py:294
  7.1 0.4 %collective-permute-start.13 = (f32[32,768]{1,0:T(8,128)S(1)}, f32[32,768]{1,0:T(8,128)S(1)}, u32[]{:S(2)}, u32[]{:S(2)}) collective-permute-start(f32[32,768]{1,0:T(8,128)S(1)} %solve_2.2.held.refs_0_), channel_id=1, source_target_pairs={{0,4},{1,5},{2,6},{3,7},{4,0},{5,1},{6,2},{7,3},{8,12},{9,13},{10,... | collective-permute-start | bytes 294920 | tf_op jit(solution)/shard_map/solved_2/ppermute | solution.py:294
  7.5 0.3 %collective-permute-done.6.refs_0_.refs_8_ = f32[32,768]{1,0:T(8,128)S(1)} collective-permute-done((f32[32,768]{1,0:T(8,128)S(1)}, f32[32,768]{1,0:T(8,128)S(1)}, u32[]{:S(2)}, u32[]{:S(2)}) %collective-permute-start.6) | collective-permute-done | bytes 98336 | tf_op jit(solution)/shard_map/beside/ppermute | solution.py:294
  7.9 0.4 %collective-permute-done.9.refs_1_.refs_9_ = f32[32,768]{1,0:T(8,128)S(1)} collective-permute-done((f32[32,768]{1,0:T(8,128)S(1)}, f32[32,768]{1,0:T(8,128)S(1)}, u32[]{:S(2)}, u32[]{:S(2)}) %collective-permute-start.9) | collective-permute-done | bytes 98336 | tf_op jit(solution)/shard_map/beside/ppermute | solution.py:294
  8.5 7.3 %collective-permute-start.12 = (f32[64,768]{1,0:T(8,128)S(1)}, f32[64,768]{1,0:T(8,128)S(1)}, u32[]{:S(2)}, u32[]{:S(2)}) collective-permute-start(f32[64,768]{1,0:T(8,128)S(1)} %product_31.1), channel_id=1, source_target_pairs={{9,13},{13,15},{15,11},{11,9},{0,4},{1,5},{2,6},{3,7},{4,0},{5,1},... | collective-permute-start | bytes 589832 | tf_op jit(solution)/shard_map/product_31/ppermute | solution.py:294
  16.0 1.2 %collective-permute-done.15.refs_0_.refs_3_.refs_11_ = f32[32,768]{1,0:T(8,128)S(1)} collective-permute-done((f32[32,768]{1,0:T(8,128)S(1)}, f32[32,768]{1,0:T(8,128)S(1)}, u32[]{:S(2)}, u32[]{:S(2)}) %collective-permute-start.15) | collective-permute-done | bytes 98336 | tf_op jit(solution)/shard_map/solved_2/ppermute | solution.py:294
  17.4 0.5 %collective-permute-start.18 = (f32[64,192]{1,0:T(8,128)S(1)}, f32[64,192]{1,0:T(8,128)S(1)}, u32[]{:S(2)}, u32[]{:S(2)}) collective-permute-start(f32[64,192]{1,0:T(8,128)S(1)} %share_2.1), channel_id=1, source_target_pairs={{2,10},{10,2},{6,14},{14,6},{0,4},{1,5},{3,7},{4,0},{5,1},{7,3},{8... | collective-permute-start | bytes 147464 | tf_op jit(solution)/shard_map/share_2/ppermute | solution.py:294
  17.8 1.2 %collective-permute-done.12.middle = f32[64,768]{1,0:T(8,128)S(1)} collective-permute-done((f32[64,768]{1,0:T(8,128)S(1)}, f32[64,768]{1,0:T(8,128)S(1)}, u32[]{:S(2)}, u32[]{:S(2)}) %collective-permute-start.12) | collective-permute-done | bytes 196640 | tf_op jit(solution)/shard_map/product_31/ppermute | solution.py:294
  19.1 0.5 %collective-permute-done.16.got = f32[32,768]{1,0:T(8,128)S(1)} collective-permute-done((f32[32,768]{1,0:T(8,128)S(1)}, f32[32,768]{1,0:T(8,128)S(1)}, u32[]{:S(2)}, u32[]{:S(2)}) %collective-permute-start.16) | collective-permute-done | bytes 98336 | tf_op jit(solution)/shard_map/product_32/ppermute | solution.py:294
  19.8 1.9 %collective-permute-start.19 = (f32[64,192]{1,0:T(8,128)S(1)}, f32[64,192]{1,0:T(8,128)S(1)}, u32[]{:S(2)}, u32[]{:S(2)}) collective-permute-start(f32[64,192]{1,0:T(8,128)S(1)} %get-tuple-element.31.refs_2_), channel_id=1, source_target_pairs={{3,7},{7,11},{11,15},{15,3},{0,4},{1,5},{2,6},{4,0},{5,1},{6,2},{8... | collective-permute-start | bytes 147464 | tf_op jit(solution)/shard_map/share_03/ppermute | solution.py:294
  21.8 0.4 %collective-permute-start.20 = (f32[64,192]{1,0:T(8,128)S(1)}, f32[64,192]{1,0:T(8,128)S(1)}, u32[]{:S(2)}, u32[]{:S(2)}) collective-permute-start(f32[64,192]{1,0:T(8,128)S(1)} %get-tuple-element.32), channel_id=1, source_target_pairs={{3,11},{11,15},{15,7},{7,3},{0,4},{1,5},{2,6},{4,0},{5,1},{6,2},{8... | collective-permute-start | bytes 147464 | tf_op jit(solution)/shard_map/share_13/ppermute | solution.py:294
  22.3 0.7 %collective-permute-done.17.refs_12_ = f32[64,192]{1,0:T(8,128)S(1)} collective-permute-done((f32[64,192]{1,0:T(8,128)S(1)}, f32[64,192]{1,0:T(8,128)S(1)}, u32[]{:S(2)}, u32[]{:S(2)}) %collective-permute-start.17) | collective-permute-done | bytes 49184 | tf_op jit(solution)/shard_map/share_3/ppermute | solution.py:294
  23.0 0.6 %collective-permute-done.19.refs_14_ = f32[64,192]{1,0:T(8,128)S(1)} collective-permute-done((f32[64,192]{1,0:T(8,128)S(1)}, f32[64,192]{1,0:T(8,128)S(1)}, u32[]{:S(2)}, u32[]{:S(2)}) %collective-permute-start.19) | collective-permute-done | bytes 49184 | tf_op jit(solution)/shard_map/share_03/ppermute | solution.py:294
  23.5 2.5 %collective-permute-done.20.refs_15_ = f32[64,192]{1,0:T(8,128)S(1)} collective-permute-done((f32[64,192]{1,0:T(8,128)S(1)}, f32[64,192]{1,0:T(8,128)S(1)}, u32[]{:S(2)}, u32[]{:S(2)}) %collective-permute-start.20) | collective-permute-done | bytes 49184 | tf_op jit(solution)/shard_map/share_13/ppermute | solution.py:294
  26.1 0.6 %copy.4 = f32[1,192,64]{1,2,0:T(8,128)} copy(f32[1,192,64]{1,2,0:T(8,128)S(1)} %bitcast.7) | data formatting | bytes 98304
  (40 shorter events, 2.1 us)
Async XLA Ops:
  0.1 1.4 %collective-permute-start = (f32[32,768]{1,0:T(8,128)S(1)}, f32[32,768]{1,0:T(8,128)S(1)}, u32[]{:S(2)}, u32[]{:S(2)}) collective-permute-start(f32[32,768]{1,0:T(8,128)S(1)} %get-tuple-element.21.held), channel_id=1, source_target_pairs={{0,4},{1,5},{2,6},{3,7},{4,0},{5,1},{6,2},{7,3},{8,12},{9,13},{10,... | collective-permute-start | bytes 294920 | tf_op jit(solution)/shard_map/solved_0/ppermute | solution.py:294
  0.1 1.5 %collective-permute-start.1 = (f32[32,768]{1,0:T(8,128)S(1)}, f32[32,768]{1,0:T(8,128)S(1)}, u32[]{:S(2)}, u32[]{:S(2)}) collective-permute-start(f32[32,768]{1,0:T(8,128)S(1)} %get-tuple-element.22.held), channel_id=1, source_target_pairs={{0,4},{1,5},{2,6},{3,7},{4,0},{5,1},{6,2},{7,3},{8,12},{9,13},{10,... | collective-permute-start | bytes 294920 | tf_op jit(solution)/shard_map/solved_0/ppermute | solution.py:294
  1.4 1.4 %collective-permute-start.2 = (f32[32,768]{1,0:T(8,128)S(1)}, f32[32,768]{1,0:T(8,128)S(1)}, u32[]{:S(2)}, u32[]{:S(2)}) collective-permute-start(f32[32,768]{1,0:T(8,128)S(1)} %product_10.2.rest_0_), channel_id=1, source_target_pairs={{0,8},{8,12},{12,14},{14,10},{10,4},{4,5},{5,1},{1,0},{2,6},{3,7},... | collective-permute-start | bytes 294920 | tf_op jit(solution)/shard_map/product_10/ppermute | solution.py:294
  1.6 2.9 %collective-permute-start.7 = (f32[32,768]{1,0:T(8,128)S(1)}, f32[32,768]{1,0:T(8,128)S(1)}, u32[]{:S(2)}, u32[]{:S(2)}) collective-permute-start(f32[32,768]{1,0:T(8,128)S(1)} %product_10.3.rest_1_), channel_id=1, source_target_pairs={{0,8},{8,12},{12,14},{14,10},{10,4},{4,5},{5,1},{1,0},{2,6},{3,7},... | collective-permute-start | bytes 294920 | tf_op jit(solution)/shard_map/product_10/ppermute | solution.py:294
  2.8 2.6 %collective-permute-start.3 = (f32[32,768]{1,0:T(8,128)S(1)}, f32[32,768]{1,0:T(8,128)S(1)}, u32[]{:S(2)}, u32[]{:S(2)}) collective-permute-start(f32[32,768]{1,0:T(8,128)S(1)} %get-tuple-element.26.held), channel_id=1, source_target_pairs={{1,5},{5,9},{9,13},{13,1},{0,4},{2,6},{3,7},{4,0},{6,2},{7,3},{8,1... | collective-permute-start | bytes 294920 | tf_op jit(solution)/shard_map/solved_1/ppermute | solution.py:294
  4.5 1.3 %collective-permute-start.4 = (f32[32,768]{1,0:T(8,128)S(1)}, f32[32,768]{1,0:T(8,128)S(1)}, u32[]{:S(2)}, u32[]{:S(2)}) collective-permute-start(f32[32,768]{1,0:T(8,128)S(1)} %get-tuple-element.27), channel_id=1, source_target_pairs={{8,9},{9,13},{13,12},{12,8},{0,4},{1,5},{2,6},{3,7},{4,0},{5,1},{6... | collective-permute-start | bytes 294920 | tf_op jit(solution)/shard_map/product_20/ppermute | solution.py:294
  4.5 1.4 %collective-permute-start.8 = (f32[32,768]{1,0:T(8,128)S(1)}, f32[32,768]{1,0:T(8,128)S(1)}, u32[]{:S(2)}, u32[]{:S(2)}) collective-permute-start(f32[32,768]{1,0:T(8,128)S(1)} %get-tuple-element.29.held), channel_id=1, source_target_pairs={{1,5},{5,9},{9,13},{13,1},{0,4},{2,6},{3,7},{4,0},{6,2},{7,3},{8,1... | collective-permute-start | bytes 294920 | tf_op jit(solution)/shard_map/solved_1/ppermute | solution.py:294
  5.0 1.3 %collective-permute-start.10 = (f32[32,768]{1,0:T(8,128)S(1)}, f32[32,768]{1,0:T(8,128)S(1)}, u32[]{:S(2)}, u32[]{:S(2)}) collective-permute-start(f32[32,768]{1,0:T(8,128)S(1)} %get-tuple-element.30), channel_id=1, source_target_pairs={{8,9},{9,13},{13,12},{12,8},{0,4},{1,5},{2,6},{3,7},{4,0},{5,1},{6... | collective-permute-start | bytes 294920 | tf_op jit(solution)/shard_map/product_20/ppermute | solution.py:294
  5.8 1.4 %collective-permute-start.5 = (f32[32,768]{1,0:T(8,128)S(1)}, f32[32,768]{1,0:T(8,128)S(1)}, u32[]{:S(2)}, u32[]{:S(2)}) collective-permute-start(f32[32,768]{1,0:T(8,128)S(1)} %join_2.2.held), channel_id=1, source_target_pairs={{2,8},{8,12},{12,13},{13,9},{9,10},{10,14},{14,6},{6,2},{0,4},{1,5... | collective-permute-start | bytes 294920 | tf_op jit(solution)/shard_map/product_21/ppermute | solution.py:294
  6.4 1.9 %collective-permute-start.11 = (f32[32,768]{1,0:T(8,128)S(1)}, f32[32,768]{1,0:T(8,128)S(1)}, u32[]{:S(2)}, u32[]{:S(2)}) collective-permute-start(f32[32,768]{1,0:T(8,128)S(1)} %join_2.3.held), channel_id=1, source_target_pairs={{2,8},{8,12},{12,13},{13,9},{9,10},{10,14},{14,6},{6,2},{0,4},{1,5... | collective-permute-start | bytes 294920 | tf_op jit(solution)/shard_map/product_21/ppermute | solution.py:294
  6.6 1.3 %collective-permute-start.6 = (f32[32,768]{1,0:T(8,128)S(1)}, f32[32,768]{1,0:T(8,128)S(1)}, u32[]{:S(2)}, u32[]{:S(2)}) collective-permute-start(f32[32,768]{1,0:T(8,128)S(1)} %collective-permute-done.3.refs_0_.refs_6_), channel_id=1, source_target_pairs={{0,4},{1,5},{2,6},{3,7},{4,0},{5,1},{6,2},{7,3},{8,12},{9,13},{10,... | collective-permute-start | bytes 294920 | tf_op jit(solution)/shard_map/beside/ppermute | solution.py:294
  6.9 1.3 %collective-permute-start.9 = (f32[32,768]{1,0:T(8,128)S(1)}, f32[32,768]{1,0:T(8,128)S(1)}, u32[]{:S(2)}, u32[]{:S(2)}) collective-permute-start(f32[32,768]{1,0:T(8,128)S(1)} %collective-permute-done.8.refs_0_.refs_7_), channel_id=1, source_target_pairs={{0,4},{1,5},{2,6},{3,7},{4,0},{5,1},{6,2},{7,3},{8,12},{9,13},{10,... | collective-permute-start | bytes 294920 | tf_op jit(solution)/shard_map/beside/ppermute | solution.py:294
  7.1 1.4 %collective-permute-start.13 = (f32[32,768]{1,0:T(8,128)S(1)}, f32[32,768]{1,0:T(8,128)S(1)}, u32[]{:S(2)}, u32[]{:S(2)}) collective-permute-start(f32[32,768]{1,0:T(8,128)S(1)} %solve_2.2.held.refs_0_), channel_id=1, source_target_pairs={{0,4},{1,5},{2,6},{3,7},{4,0},{5,1},{6,2},{7,3},{8,12},{9,13},{10,... | collective-permute-start | bytes 294920 | tf_op jit(solution)/shard_map/solved_2/ppermute | solution.py:294
  8.5 10.5 %collective-permute-start.12 = (f32[64,768]{1,0:T(8,128)S(1)}, f32[64,768]{1,0:T(8,128)S(1)}, u32[]{:S(2)}, u32[]{:S(2)}) collective-permute-start(f32[64,768]{1,0:T(8,128)S(1)} %product_31.1), channel_id=1, source_target_pairs={{9,13},{13,15},{15,11},{11,9},{0,4},{1,5},{2,6},{3,7},{4,0},{5,1},... | collective-permute-start | bytes 589832 | tf_op jit(solution)/shard_map/product_31/ppermute | solution.py:294
  15.9 1.4 %collective-permute-start.15 = (f32[32,768]{1,0:T(8,128)S(1)}, f32[32,768]{1,0:T(8,128)S(1)}, u32[]{:S(2)}, u32[]{:S(2)}) collective-permute-start(f32[32,768]{1,0:T(8,128)S(1)} %solve_2.3.held.refs_1_), channel_id=1, source_target_pairs={{0,4},{1,5},{2,6},{3,7},{4,0},{5,1},{6,2},{7,3},{8,12},{9,13},{10,... | collective-permute-start | bytes 294920 | tf_op jit(solution)/shard_map/solved_2/ppermute | solution.py:294
  15.9 3.1 %collective-permute-start.14 = (f32[32,768]{1,0:T(8,128)S(1)}, f32[32,768]{1,0:T(8,128)S(1)}, u32[]{:S(2)}, u32[]{:S(2)}) collective-permute-start(f32[32,768]{1,0:T(8,128)S(1)} %product_32.2.after), channel_id=1, source_target_pairs={{2,10},{10,14},{14,15},{15,11},{11,7},{7,3},{3,6},{6,2},{0,4},{1,5... | collective-permute-start | bytes 294920 | tf_op jit(solution)/shard_map/product_32/ppermute | solution.py:294
  17.2 2.3 %collective-permute-start.16 = (f32[32,768]{1,0:T(8,128)S(1)}, f32[32,768]{1,0:T(8,128)S(1)}, u32[]{:S(2)}, u32[]{:S(2)}) collective-permute-start(f32[32,768]{1,0:T(8,128)S(1)} %product_32.3), channel_id=1, source_target_pairs={{2,10},{10,14},{14,15},{15,11},{11,7},{7,3},{3,6},{6,2},{0,4},{1,5... | collective-permute-start | bytes 294920 | tf_op jit(solution)/shard_map/product_32/ppermute | solution.py:294
  17.4 4.9 %collective-permute-start.18 = (f32[64,192]{1,0:T(8,128)S(1)}, f32[64,192]{1,0:T(8,128)S(1)}, u32[]{:S(2)}, u32[]{:S(2)}) collective-permute-start(f32[64,192]{1,0:T(8,128)S(1)} %share_2.1), channel_id=1, source_target_pairs={{2,10},{10,2},{6,14},{14,6},{0,4},{1,5},{3,7},{4,0},{5,1},{7,3},{8... | collective-permute-start | bytes 147464 | tf_op jit(solution)/shard_map/share_2/ppermute | solution.py:294
  19.8 3.7 %collective-permute-start.19 = (f32[64,192]{1,0:T(8,128)S(1)}, f32[64,192]{1,0:T(8,128)S(1)}, u32[]{:S(2)}, u32[]{:S(2)}) collective-permute-start(f32[64,192]{1,0:T(8,128)S(1)} %get-tuple-element.31.refs_2_), channel_id=1, source_target_pairs={{3,7},{7,11},{11,15},{15,3},{0,4},{1,5},{2,6},{4,0},{5,1},{6,2},{8... | collective-permute-start | bytes 147464 | tf_op jit(solution)/shard_map/share_03/ppermute | solution.py:294
  21.7 1.3 %collective-permute-start.17 = (f32[64,192]{1,0:T(8,128)S(1)}, f32[64,192]{1,0:T(8,128)S(1)}, u32[]{:S(2)}, u32[]{:S(2)}) collective-permute-start(f32[64,192]{1,0:T(8,128)S(1)} %across_3.1), channel_id=1, source_target_pairs={{0,4},{1,5},{2,6},{3,7},{4,0},{5,1},{6,2},{7,3},{8,12},{9,13},{10,... | collective-permute-start | bytes 147464 | tf_op jit(solution)/shard_map/share_3/ppermute | solution.py:294
  21.8 4.3 %collective-permute-start.20 = (f32[64,192]{1,0:T(8,128)S(1)}, f32[64,192]{1,0:T(8,128)S(1)}, u32[]{:S(2)}, u32[]{:S(2)}) collective-permute-start(f32[64,192]{1,0:T(8,128)S(1)} %get-tuple-element.32), channel_id=1, source_target_pairs={{3,11},{11,15},{15,7},{7,3},{0,4},{1,5},{2,6},{4,0},{5,1},{6,2},{8... | collective-permute-start | bytes 147464 | tf_op jit(solution)/shard_map/share_13/ppermute | solution.py:294

commit v6 on v5

--- a/solution.py
+++ b/solution.py
@@ -282,7 +282,7 @@
     "product_31": route([(2, 1), (3, 1), (3, 3), (2, 3)]),
     "solved_2": route(),
     "product_32": route([(0, 2), (2, 2), (3, 2), (3, 3), (2, 3), (1, 3), (0, 3), (1, 2)]),
-    "share_2": route([(0, 2), (2, 2)], [(1, 2), (3, 2)]),
+    "share_2": [(2 * SIDE + 2, 2), (3 * SIDE + 2, SIDE + 2)],
     "share_3": route(),
     "share_03": route([(0, 3), (1, 3), (2, 3), (3, 3)]),
     "share_13": route([(0, 3), (2, 3), (3, 3), (1, 3)]),

time: 26.9 us -> 26.9 us (level)
  no operation moved by 1% of the time
where the time goes in v6:
time: 26.9 us; the launch traced here: 26.7 us
  starting transfers between devices  15.4 us (57%)
  waiting for transfers between devices  10 us (37%)
  local copies, waits for them, and re-layouts  0.63 us (2%)
  Pallas kernels  0.52 us (2%)
    ppermute x21, starting transfers between devices, send(): return lax.ppermute(array, GRID, ROUTES[name])  15.4 us
    ppermute x21, waiting for transfers between devices, send(): return lax.ppermute(array, GRID, ROUTES[name])  10 us
    unnamed x1, local copies, waits for them, and re-layouts  0.63 us
  transfers between devices with their start and end apart: 21, of which 15 were waited for; matrix products, arithmetic and copies ran while one was open for 0% of the time, Pallas kernels for 2%

profile of v6, /device:TPU:30, one launch (start us, length us, event | category | flops | bytes accessed | tf_op | source)
XLA Modules:
  0.0 26.7 jit_solution(17966123121526716624)
XLA Ops:
  0.1 0.5 %collective-permute-start.1 = (f32[32,768]{1,0:T(8,128)S(1)}, f32[32,768]{1,0:T(8,128)S(1)}, u32[]{:S(2)}, u32[]{:S(2)}) collective-permute-start(f32[32,768]{1,0:T(8,128)S(1)} %get-tuple-element.22.held), channel_id=1, source_target_pairs={{0,4},{1,5},{2,6},{3,7},{4,0},{5,1},{6,2},{7,3},{8,12},{9,13},{10,... | collective-permute-start | bytes 294920 | tf_op jit(solution)/shard_map/solved_0/ppermute | solution.py:294
  0.6 0.8 %collective-permute-done.refs_0_.refs_2_ = f32[32,768]{1,0:T(8,128)S(1)} collective-permute-done((f32[32,768]{1,0:T(8,128)S(1)}, f32[32,768]{1,0:T(8,128)S(1)}, u32[]{:S(2)}, u32[]{:S(2)}) %collective-permute-start) | collective-permute-done | bytes 98336 | tf_op jit(solution)/shard_map/solved_0/ppermute | solution.py:294
  1.6 0.5 %collective-permute-start.7 = (f32[32,768]{1,0:T(8,128)S(1)}, f32[32,768]{1,0:T(8,128)S(1)}, u32[]{:S(2)}, u32[]{:S(2)}) collective-permute-start(f32[32,768]{1,0:T(8,128)S(1)} %product_10.3.rest_1_), channel_id=1, source_target_pairs={{0,8},{8,12},{12,14},{14,10},{10,4},{4,5},{5,1},{1,0},{2,6},{3,7},... | collective-permute-start | bytes 294920 | tf_op jit(solution)/shard_map/product_10/ppermute | solution.py:294
  2.1 0.7 %collective-permute-done.2.second.refs_4_ = f32[32,768]{1,0:T(8,128)S(1)} collective-permute-done((f32[32,768]{1,0:T(8,128)S(1)}, f32[32,768]{1,0:T(8,128)S(1)}, u32[]{:S(2)}, u32[]{:S(2)}) %collective-permute-start.2) | collective-permute-done | bytes 98336 | tf_op jit(solution)/shard_map/product_10/ppermute | solution.py:294
  2.8 1.6 %collective-permute-start.3 = (f32[32,768]{1,0:T(8,128)S(1)}, f32[32,768]{1,0:T(8,128)S(1)}, u32[]{:S(2)}, u32[]{:S(2)}) collective-permute-start(f32[32,768]{1,0:T(8,128)S(1)} %get-tuple-element.26.held), channel_id=1, source_target_pairs={{1,5},{5,9},{9,13},{13,1},{0,4},{2,6},{3,7},{4,0},{6,2},{7,3},{8,1... | collective-permute-start | bytes 294920 | tf_op jit(solution)/shard_map/solved_1/ppermute | solution.py:294
  4.5 0.5 %collective-permute-start.8 = (f32[32,768]{1,0:T(8,128)S(1)}, f32[32,768]{1,0:T(8,128)S(1)}, u32[]{:S(2)}, u32[]{:S(2)}) collective-permute-start(f32[32,768]{1,0:T(8,128)S(1)} %get-tuple-element.29.held), channel_id=1, source_target_pairs={{1,5},{5,9},{9,13},{13,1},{0,4},{2,6},{3,7},{4,0},{6,2},{7,3},{8,1... | collective-permute-start | bytes 294920 | tf_op jit(solution)/shard_map/solved_1/ppermute | solution.py:294
  5.1 0.3 %collective-permute-done.3.refs_0_.refs_6_ = f32[32,768]{1,0:T(8,128)S(1)} collective-permute-done((f32[32,768]{1,0:T(8,128)S(1)}, f32[32,768]{1,0:T(8,128)S(1)}, u32[]{:S(2)}, u32[]{:S(2)}) %collective-permute-start.3) | collective-permute-done | bytes 98336 | tf_op jit(solution)/shard_map/solved_1/ppermute | solution.py:294
  5.4 0.3 %collective-permute-done.4.side = f32[32,768]{1,0:T(8,128)S(1)} collective-permute-done((f32[32,768]{1,0:T(8,128)S(1)}, f32[32,768]{1,0:T(8,128)S(1)}, u32[]{:S(2)}, u32[]{:S(2)}) %collective-permute-start.4) | collective-permute-done | bytes 98336 | tf_op jit(solution)/shard_map/product_20/ppermute | solution.py:294
  6.0 0.3 %collective-permute-done.10.side = f32[32,768]{1,0:T(8,128)S(1)} collective-permute-done((f32[32,768]{1,0:T(8,128)S(1)}, f32[32,768]{1,0:T(8,128)S(1)}, u32[]{:S(2)}, u32[]{:S(2)}) %collective-permute-start.10) | collective-permute-done | bytes 98336 | tf_op jit(solution)/shard_map/product_20/ppermute | solution.py:294
  6.6 0.4 %collective-permute-start.6 = (f32[32,768]{1,0:T(8,128)S(1)}, f32[32,768]{1,0:T(8,128)S(1)}, u32[]{:S(2)}, u32[]{:S(2)}) collective-permute-start(f32[32,768]{1,0:T(8,128)S(1)} %collective-permute-done.3.refs_0_.refs_6_), channel_id=1, source_target_pairs={{0,4},{1,5},{2,6},{3,7},{4,0},{5,1},{6,2},{7,3},{8,12},{9,13},{10,... | collective-permute-start | bytes 294920 | tf_op jit(solution)/shard_map/beside/ppermute | solution.py:294
  7.1 0.4 %collective-permute-start.13 = (f32[32,768]{1,0:T(8,128)S(1)}, f32[32,768]{1,0:T(8,128)S(1)}, u32[]{:S(2)}, u32[]{:S(2)}) collective-permute-start(f32[32,768]{1,0:T(8,128)S(1)} %solve_2.2.held.refs_0_), channel_id=1, source_target_pairs={{0,4},{1,5},{2,6},{3,7},{4,0},{5,1},{6,2},{7,3},{8,12},{9,13},{10,... | collective-permute-start | bytes 294920 | tf_op jit(solution)/shard_map/solved_2/ppermute | solution.py:294
  7.5 0.3 %collective-permute-done.6.refs_0_.refs_8_ = f32[32,768]{1,0:T(8,128)S(1)} collective-permute-done((f32[32,768]{1,0:T(8,128)S(1)}, f32[32,768]{1,0:T(8,128)S(1)}, u32[]{:S(2)}, u32[]{:S(2)}) %collective-permute-start.6) | collective-permute-done | bytes 98336 | tf_op jit(solution)/shard_map/beside/ppermute | solution.py:294
  7.9 0.4 %collective-permute-done.9.refs_1_.refs_9_ = f32[32,768]{1,0:T(8,128)S(1)} collective-permute-done((f32[32,768]{1,0:T(8,128)S(1)}, f32[32,768]{1,0:T(8,128)S(1)}, u32[]{:S(2)}, u32[]{:S(2)}) %collective-permute-start.9) | collective-permute-done | bytes 98336 | tf_op jit(solution)/shard_map/beside/ppermute | solution.py:294
  8.5 7.3 %collective-permute-start.12 = (f32[64,768]{1,0:T(8,128)S(1)}, f32[64,768]{1,0:T(8,128)S(1)}, u32[]{:S(2)}, u32[]{:S(2)}) collective-permute-start(f32[64,768]{1,0:T(8,128)S(1)} %product_31.1), channel_id=1, source_target_pairs={{9,13},{13,15},{15,11},{11,9},{0,4},{1,5},{2,6},{3,7},{4,0},{5,1},... | collective-permute-start | bytes 589832 | tf_op jit(solution)/shard_map/product_31/ppermute | solution.py:294
  16.0 1.2 %collective-permute-done.15.refs_0_.refs_3_.refs_11_ = f32[32,768]{1,0:T(8,128)S(1)} collective-permute-done((f32[32,768]{1,0:T(8,128)S(1)}, f32[32,768]{1,0:T(8,128)S(1)}, u32[]{:S(2)}, u32[]{:S(2)}) %collective-permute-start.15) | collective-permute-done | bytes 98336 | tf_op jit(solution)/shard_map/solved_2/ppermute | solution.py:294
  17.4 0.7 %collective-permute-start.18 = (f32[64,192]{1,0:T(8,128)S(1)}, f32[64,192]{1,0:T(8,128)S(1)}, u32[]{:S(2)}, u32[]{:S(2)}) collective-permute-start(f32[64,192]{1,0:T(8,128)S(1)} %share_2.1), channel_id=1, source_target_pairs={{10,2},{14,6},{26,18},{30,22}} | collective-permute-start | bytes 147464 | tf_op jit(solution)/shard_map/share_2/ppermute | solution.py:294
  18.0 1.0 %collective-permute-done.12.middle = f32[64,768]{1,0:T(8,128)S(1)} collective-permute-done((f32[64,768]{1,0:T(8,128)S(1)}, f32[64,768]{1,0:T(8,128)S(1)}, u32[]{:S(2)}, u32[]{:S(2)}) %collective-permute-start.12) | collective-permute-done | bytes 196640 | tf_op jit(solution)/shard_map/product_31/ppermute | solution.py:294
  19.1 0.5 %collective-permute-done.16.got = f32[32,768]{1,0:T(8,128)S(1)} collective-permute-done((f32[32,768]{1,0:T(8,128)S(1)}, f32[32,768]{1,0:T(8,128)S(1)}, u32[]{:S(2)}, u32[]{:S(2)}) %collective-permute-start.16) | collective-permute-done | bytes 98336 | tf_op jit(solution)/shard_map/product_32/ppermute | solution.py:294
  19.8 1.9 %collective-permute-start.19 = (f32[64,192]{1,0:T(8,128)S(1)}, f32[64,192]{1,0:T(8,128)S(1)}, u32[]{:S(2)}, u32[]{:S(2)}) collective-permute-start(f32[64,192]{1,0:T(8,128)S(1)} %get-tuple-element.31.refs_2_), channel_id=1, source_target_pairs={{3,7},{7,11},{11,15},{15,3},{0,4},{1,5},{2,6},{4,0},{5,1},{6,2},{8... | collective-permute-start | bytes 147464 | tf_op jit(solution)/shard_map/share_03/ppermute | solution.py:294
  21.8 0.4 %collective-permute-start.20 = (f32[64,192]{1,0:T(8,128)S(1)}, f32[64,192]{1,0:T(8,128)S(1)}, u32[]{:S(2)}, u32[]{:S(2)}) collective-permute-start(f32[64,192]{1,0:T(8,128)S(1)} %get-tuple-element.32), channel_id=1, source_target_pairs={{3,11},{11,15},{15,7},{7,3},{0,4},{1,5},{2,6},{4,0},{5,1},{6,2},{8... | collective-permute-start | bytes 147464 | tf_op jit(solution)/shard_map/share_13/ppermute | solution.py:294
  22.3 0.7 %collective-permute-done.17.refs_12_ = f32[64,192]{1,0:T(8,128)S(1)} collective-permute-done((f32[64,192]{1,0:T(8,128)S(1)}, f32[64,192]{1,0:T(8,128)S(1)}, u32[]{:S(2)}, u32[]{:S(2)}) %collective-permute-start.17) | collective-permute-done | bytes 49184 | tf_op jit(solution)/shard_map/share_3/ppermute | solution.py:294
  23.0 0.6 %collective-permute-done.19.refs_14_ = f32[64,192]{1,0:T(8,128)S(1)} collective-permute-done((f32[64,192]{1,0:T(8,128)S(1)}, f32[64,192]{1,0:T(8,128)S(1)}, u32[]{:S(2)}, u32[]{:S(2)}) %collective-permute-start.19) | collective-permute-done | bytes 49184 | tf_op jit(solution)/shard_map/share_03/ppermute | solution.py:294
  23.5 2.5 %collective-permute-done.20.refs_15_ = f32[64,192]{1,0:T(8,128)S(1)} collective-permute-done((f32[64,192]{1,0:T(8,128)S(1)}, f32[64,192]{1,0:T(8,128)S(1)}, u32[]{:S(2)}, u32[]{:S(2)}) %collective-permute-start.20) | collective-permute-done | bytes 49184 | tf_op jit(solution)/shard_map/share_13/ppermute | solution.py:294
  26.1 0.6 %copy.4 = f32[1,192,64]{1,2,0:T(8,128)} copy(f32[1,192,64]{1,2,0:T(8,128)S(1)} %bitcast.7) | data formatting | bytes 98304
  (40 shorter events, 2.1 us)
Async XLA Ops:
  0.1 1.4 %collective-permute-start = (f32[32,768]{1,0:T(8,128)S(1)}, f32[32,768]{1,0:T(8,128)S(1)}, u32[]{:S(2)}, u32[]{:S(2)}) collective-permute-start(f32[32,768]{1,0:T(8,128)S(1)} %get-tuple-element.21.held), channel_id=1, source_target_pairs={{0,4},{1,5},{2,6},{3,7},{4,0},{5,1},{6,2},{7,3},{8,12},{9,13},{10,... | collective-permute-start | bytes 294920 | tf_op jit(solution)/shard_map/solved_0/ppermute | solution.py:294
  0.1 1.5 %collective-permute-start.1 = (f32[32,768]{1,0:T(8,128)S(1)}, f32[32,768]{1,0:T(8,128)S(1)}, u32[]{:S(2)}, u32[]{:S(2)}) collective-permute-start(f32[32,768]{1,0:T(8,128)S(1)} %get-tuple-element.22.held), channel_id=1, source_target_pairs={{0,4},{1,5},{2,6},{3,7},{4,0},{5,1},{6,2},{7,3},{8,12},{9,13},{10,... | collective-permute-start | bytes 294920 | tf_op jit(solution)/shard_map/solved_0/ppermute | solution.py:294
  1.4 1.4 %collective-permute-start.2 = (f32[32,768]{1,0:T(8,128)S(1)}, f32[32,768]{1,0:T(8,128)S(1)}, u32[]{:S(2)}, u32[]{:S(2)}) collective-permute-start(f32[32,768]{1,0:T(8,128)S(1)} %product_10.2.rest_0_), channel_id=1, source_target_pairs={{0,8},{8,12},{12,14},{14,10},{10,4},{4,5},{5,1},{1,0},{2,6},{3,7},... | collective-permute-start | bytes 294920 | tf_op jit(solution)/shard_map/product_10/ppermute | solution.py:294
  1.6 2.9 %collective-permute-start.7 = (f32[32,768]{1,0:T(8,128)S(1)}, f32[32,768]{1,0:T(8,128)S(1)}, u32[]{:S(2)}, u32[]{:S(2)}) collective-permute-start(f32[32,768]{1,0:T(8,128)S(1)} %product_10.3.rest_1_), channel_id=1, source_target_pairs={{0,8},{8,12},{12,14},{14,10},{10,4},{4,5},{5,1},{1,0},{2,6},{3,7},... | collective-permute-start | bytes 294920 | tf_op jit(solution)/shard_map/product_10/ppermute | solution.py:294
  2.8 2.6 %collective-permute-start.3 = (f32[32,768]{1,0:T(8,128)S(1)}, f32[32,768]{1,0:T(8,128)S(1)}, u32[]{:S(2)}, u32[]{:S(2)}) collective-permute-start(f32[32,768]{1,0:T(8,128)S(1)} %get-tuple-element.26.held), channel_id=1, source_target_pairs={{1,5},{5,9},{9,13},{13,1},{0,4},{2,6},{3,7},{4,0},{6,2},{7,3},{8,1... | collective-permute-start | bytes 294920 | tf_op jit(solution)/shard_map/solved_1/ppermute | solution.py:294
  4.5 1.3 %collective-permute-start.4 = (f32[32,768]{1,0:T(8,128)S(1)}, f32[32,768]{1,0:T(8,128)S(1)}, u32[]{:S(2)}, u32[]{:S(2)}) collective-permute-start(f32[32,768]{1,0:T(8,128)S(1)} %get-tuple-element.27), channel_id=1, source_target_pairs={{8,9},{9,13},{13,12},{12,8},{0,4},{1,5},{2,6},{3,7},{4,0},{5,1},{6... | collective-permute-start | bytes 294920 | tf_op jit(solution)/shard_map/product_20/ppermute | solution.py:294
  4.5 1.4 %collective-permute-start.8 = (f32[32,768]{1,0:T(8,128)S(1)}, f32[32,768]{1,0:T(8,128)S(1)}, u32[]{:S(2)}, u32[]{:S(2)}) collective-permute-start(f32[32,768]{1,0:T(8,128)S(1)} %get-tuple-element.29.held), channel_id=1, source_target_pairs={{1,5},{5,9},{9,13},{13,1},{0,4},{2,6},{3,7},{4,0},{6,2},{7,3},{8,1... | collective-permute-start | bytes 294920 | tf_op jit(solution)/shard_map/solved_1/ppermute | solution.py:294
  5.0 1.3 %collective-permute-start.10 = (f32[32,768]{1,0:T(8,128)S(1)}, f32[32,768]{1,0:T(8,128)S(1)}, u32[]{:S(2)}, u32[]{:S(2)}) collective-permute-start(f32[32,768]{1,0:T(8,128)S(1)} %get-tuple-element.30), channel_id=1, source_target_pairs={{8,9},{9,13},{13,12},{12,8},{0,4},{1,5},{2,6},{3,7},{4,0},{5,1},{6... | collective-permute-start | bytes 294920 | tf_op jit(solution)/shard_map/product_20/ppermute | solution.py:294
  5.8 1.4 %collective-permute-start.5 = (f32[32,768]{1,0:T(8,128)S(1)}, f32[32,768]{1,0:T(8,128)S(1)}, u32[]{:S(2)}, u32[]{:S(2)}) collective-permute-start(f32[32,768]{1,0:T(8,128)S(1)} %join_2.2.held), channel_id=1, source_target_pairs={{2,8},{8,12},{12,13},{13,9},{9,10},{10,14},{14,6},{6,2},{0,4},{1,5... | collective-permute-start | bytes 294920 | tf_op jit(solution)/shard_map/product_21/ppermute | solution.py:294
  6.4 1.9 %collective-permute-start.11 = (f32[32,768]{1,0:T(8,128)S(1)}, f32[32,768]{1,0:T(8,128)S(1)}, u32[]{:S(2)}, u32[]{:S(2)}) collective-permute-start(f32[32,768]{1,0:T(8,128)S(1)} %join_2.3.held), channel_id=1, source_target_pairs={{2,8},{8,12},{12,13},{13,9},{9,10},{10,14},{14,6},{6,2},{0,4},{1,5... | collective-permute-start | bytes 294920 | tf_op jit(solution)/shard_map/product_21/ppermute | solution.py:294
  6.6 1.3 %collective-permute-start.6 = (f32[32,768]{1,0:T(8,128)S(1)}, f32[32,768]{1,0:T(8,128)S(1)}, u32[]{:S(2)}, u32[]{:S(2)}) collective-permute-start(f32[32,768]{1,0:T(8,128)S(1)} %collective-permute-done.3.refs_0_.refs_6_), channel_id=1, source_target_pairs={{0,4},{1,5},{2,6},{3,7},{4,0},{5,1},{6,2},{7,3},{8,12},{9,13},{10,... | collective-permute-start | bytes 294920 | tf_op jit(solution)/shard_map/beside/ppermute | solution.py:294
  6.9 1.3 %collective-permute-start.9 = (f32[32,768]{1,0:T(8,128)S(1)}, f32[32,768]{1,0:T(8,128)S(1)}, u32[]{:S(2)}, u32[]{:S(2)}) collective-permute-start(f32[32,768]{1,0:T(8,128)S(1)} %collective-permute-done.8.refs_0_.refs_7_), channel_id=1, source_target_pairs={{0,4},{1,5},{2,6},{3,7},{4,0},{5,1},{6,2},{7,3},{8,12},{9,13},{10,... | collective-permute-start | bytes 294920 | tf_op jit(solution)/shard_map/beside/ppermute | solution.py:294
  7.1 1.4 %collective-permute-start.13 = (f32[32,768]{1,0:T(8,128)S(1)}, f32[32,768]{1,0:T(8,128)S(1)}, u32[]{:S(2)}, u32[]{:S(2)}) collective-permute-start(f32[32,768]{1,0:T(8,128)S(1)} %solve_2.2.held.refs_0_), channel_id=1, source_target_pairs={{0,4},{1,5},{2,6},{3,7},{4,0},{5,1},{6,2},{7,3},{8,12},{9,13},{10,... | collective-permute-start | bytes 294920 | tf_op jit(solution)/shard_map/solved_2/ppermute | solution.py:294
  8.5 10.5 %collective-permute-start.12 = (f32[64,768]{1,0:T(8,128)S(1)}, f32[64,768]{1,0:T(8,128)S(1)}, u32[]{:S(2)}, u32[]{:S(2)}) collective-permute-start(f32[64,768]{1,0:T(8,128)S(1)} %product_31.1), channel_id=1, source_target_pairs={{9,13},{13,15},{15,11},{11,9},{0,4},{1,5},{2,6},{3,7},{4,0},{5,1},... | collective-permute-start | bytes 589832 | tf_op jit(solution)/shard_map/product_31/ppermute | solution.py:294
  15.9 1.4 %collective-permute-start.15 = (f32[32,768]{1,0:T(8,128)S(1)}, f32[32,768]{1,0:T(8,128)S(1)}, u32[]{:S(2)}, u32[]{:S(2)}) collective-permute-start(f32[32,768]{1,0:T(8,128)S(1)} %solve_2.3.held.refs_1_), channel_id=1, source_target_pairs={{0,4},{1,5},{2,6},{3,7},{4,0},{5,1},{6,2},{7,3},{8,12},{9,13},{10,... | collective-permute-start | bytes 294920 | tf_op jit(solution)/shard_map/solved_2/ppermute | solution.py:294
  15.9 3.1 %collective-permute-start.14 = (f32[32,768]{1,0:T(8,128)S(1)}, f32[32,768]{1,0:T(8,128)S(1)}, u32[]{:S(2)}, u32[]{:S(2)}) collective-permute-start(f32[32,768]{1,0:T(8,128)S(1)} %product_32.2.after), channel_id=1, source_target_pairs={{2,10},{10,14},{14,15},{15,11},{11,7},{7,3},{3,6},{6,2},{0,4},{1,5... | collective-permute-start | bytes 294920 | tf_op jit(solution)/shard_map/product_32/ppermute | solution.py:294
  17.2 2.3 %collective-permute-start.16 = (f32[32,768]{1,0:T(8,128)S(1)}, f32[32,768]{1,0:T(8,128)S(1)}, u32[]{:S(2)}, u32[]{:S(2)}) collective-permute-start(f32[32,768]{1,0:T(8,128)S(1)} %product_32.3), channel_id=1, source_target_pairs={{2,10},{10,14},{14,15},{15,11},{11,7},{7,3},{3,6},{6,2},{0,4},{1,5... | collective-permute-start | bytes 294920 | tf_op jit(solution)/shard_map/product_32/ppermute | solution.py:294
  17.4 4.9 %collective-permute-start.18 = (f32[64,192]{1,0:T(8,128)S(1)}, f32[64,192]{1,0:T(8,128)S(1)}, u32[]{:S(2)}, u32[]{:S(2)}) collective-permute-start(f32[64,192]{1,0:T(8,128)S(1)} %share_2.1), channel_id=1, source_target_pairs={{10,2},{14,6},{26,18},{30,22}} | collective-permute-start | bytes 147464 | tf_op jit(solution)/shard_map/share_2/ppermute | solution.py:294
  19.8 3.7 %collective-permute-start.19 = (f32[64,192]{1,0:T(8,128)S(1)}, f32[64,192]{1,0:T(8,128)S(1)}, u32[]{:S(2)}, u32[]{:S(2)}) collective-permute-start(f32[64,192]{1,0:T(8,128)S(1)} %get-tuple-element.31.refs_2_), channel_id=1, source_target_pairs={{3,7},{7,11},{11,15},{15,3},{0,4},{1,5},{2,6},{4,0},{5,1},{6,2},{8... | collective-permute-start | bytes 147464 | tf_op jit(solution)/shard_map/share_03/ppermute | solution.py:294
  21.7 1.3 %collective-permute-start.17 = (f32[64,192]{1,0:T(8,128)S(1)}, f32[64,192]{1,0:T(8,128)S(1)}, u32[]{:S(2)}, u32[]{:S(2)}) collective-permute-start(f32[64,192]{1,0:T(8,128)S(1)} %across_3.1), channel_id=1, source_target_pairs={{0,4},{1,5},{2,6},{3,7},{4,0},{5,1},{6,2},{7,3},{8,12},{9,13},{10,... | collective-permute-start | bytes 147464 | tf_op jit(solution)/shard_map/share_3/ppermute | solution.py:294
  21.8 4.3 %collective-permute-start.20 = (f32[64,192]{1,0:T(8,128)S(1)}, f32[64,192]{1,0:T(8,128)S(1)}, u32[]{:S(2)}, u32[]{:S(2)}) collective-permute-start(f32[64,192]{1,0:T(8,128)S(1)} %get-tuple-element.32), channel_id=1, source_target_pairs={{3,11},{11,15},{15,7},{7,3},{0,4},{1,5},{2,6},{4,0},{5,1},{6,2},{8... | collective-permute-start | bytes 147464 | tf_op jit(solution)/shard_map/share_13/ppermute | solution.py:294
